TPU v7x, 256 devices: a whole 4x4x8 slice. The times are simulated.
256 devices in a mesh: inst: 4 (over x), section: 8 (over z_lo, core), tp: 8 (over y, z_hi).
Axes of the slice: x: 4, y: 4, z: 8 (z_hi: 2, z_lo: 4; z = z_hi * 4 + z_lo), core: 2. Of those that a mesh axis runs over, the one named last changes fastest.
Arguments:
- hidden: bfloat16 [64, 8192], P('inst', 'tp'), may hold values from -6 to 6
- queries: bfloat16 [8, 64, 4096], P('section', 'inst', 'tp'), may hold values from -32 to 32
- new_kv: bfloat16 [8, 64, 2048], P('section', 'inst', 'tp'), may hold values from -12 to 12
- kv_cache: bfloat16 [8, 64, 8, 512, 256], P('section', 'inst', 'tp'), may hold values from -64 to 64
- lengths: int32 [64], P('inst'), may hold values from 1 to 512, as said below
- anchor: int32 [64], replicated, may hold values from 0 to 63, as said below
- out_weight: bfloat16 [8, 4096, 8192], P('section', 'tp'), may hold values from -0.09375 to 0.09375
Outputs:
- layer_outputs: bfloat16 [8, 64, 8192], P('section', 'inst', 'tp')
- moved_cache: bfloat16 [8, 64, 8, 512, 256], P('section', 'inst', 'tp')
- moved_len: int32 [64], P('inst')
Inputs may be any that keep to these rules, and one draw needn't show every extreme that they name: anchor is a permutation of all 64 slots; each instance receives exactly 2 requests from each other instance and keeps the rest of its own. `lengths`: some request has exactly 512 positions.
All inputs are finite; a program needn't handle non-finite values.
Results may differ from a plain program's by a relative error of at most 0.0095.
Values may be sent and summed in bfloat16 or wider, within the bound.
A program may use at most 128 MiB of HBM per device.

v0:
```python
import math

import jax
import jax.numpy as jnp
from jax import lax
from jax.sharding import PartitionSpec as P

MIG = 2


def shifted(value, axis, steps):
    count = lax.axis_size(axis)
    first, last = (max(0, -steps), min(count, count - steps))
    return lax.ppermute(value, axis, [(source, source + steps) for source in range(first, last)])


def attend(query_rows, pair_rows, cache_rows, live_len, heads_kv):
    item_count = query_rows.shape[0]
    head_dim = cache_rows.shape[-1] // 2
    query = query_rows.reshape(item_count, heads_kv, -1, head_dim)
    new_pair = pair_rows.reshape(item_count, heads_kv, 2 * head_dim)
    inv_root = 1.0 / math.sqrt(head_dim)
    scores = (
        jnp.einsum(
            "rkqd,rkpd->rkqp", query, cache_rows[..., :head_dim], preferred_element_type=jnp.float32
        )
        * inv_root
    )
    positions = jnp.arange(cache_rows.shape[2], dtype=jnp.int32)
    live = positions[None, None, None, :] < live_len[:, None, None, None]
    scores = jnp.where(live, scores, -jnp.inf)
    new_score = (
        jnp.einsum(
            "rkqd,rkd->rkq", query, new_pair[..., :head_dim], preferred_element_type=jnp.float32
        )
        * inv_root
    )
    row_max = jnp.maximum(jnp.max(scores, axis=-1), new_score)
    expo = jnp.exp(scores - row_max[..., None])
    new_expo = jnp.exp(new_score - row_max)
    summed = jnp.sum(expo, axis=-1) + new_expo
    probs = (expo / summed[..., None]).astype(jnp.bfloat16)
    new_prob = (new_expo / summed).astype(jnp.bfloat16)
    result = jnp.einsum(
        "rkqp,rkpd->rkqd", probs, cache_rows[..., head_dim:], preferred_element_type=jnp.float32
    )
    result = result + new_prob.astype(jnp.float32)[..., None] * new_pair[
        :, :, None, head_dim:
    ].astype(jnp.float32)
    return result.astype(jnp.bfloat16).reshape(item_count, -1)


def body(hidden, queries, new_kv, kv_cache, lengths, anchor, out_weight):
    inst_count = lax.axis_size("inst")
    own_inst = lax.axis_index("inst")
    slot_count = hidden.shape[0]
    heads_kv = kv_cache.shape[2]
    depth = kv_cache.shape[3]
    wide = kv_cache.shape[4]
    cache_flat = kv_cache[0].reshape(slot_count, -1)
    query_rows = queries[0]
    pair_rows = new_kv[0]
    slot_ids = jnp.arange(slot_count, dtype=jnp.int32)
    move_ids = jnp.arange(MIG, dtype=jnp.int32)
    anchor_rows = anchor.reshape(inst_count, slot_count)
    from_inst = anchor_rows // slot_count
    from_slot = anchor_rows % slot_count
    my_from_inst = lax.dynamic_index_in_dim(from_inst, own_inst, 0, keepdims=False)
    my_from_slot = lax.dynamic_index_in_dim(from_slot, own_inst, 0, keepdims=False)
    is_local = my_from_inst == own_inst
    earlier_same = (my_from_inst[:, None] == my_from_inst[None, :]) & (
        slot_ids[None, :] < slot_ids[:, None]
    )
    my_rank = jnp.sum(earlier_same.astype(jnp.int32), axis=1)
    remote_pos = jnp.where(is_local, 0, my_from_inst * MIG + my_rank)
    from_me = from_inst == own_inst
    send_rank = jnp.cumsum(from_me.astype(jnp.int32), axis=1) - 1
    pick_out = from_me[:, None, :] & (send_rank[:, None, :] == move_ids[None, :, None])
    send_slot = jnp.sum(jnp.where(pick_out, from_slot[:, None, :], 0), axis=-1).reshape(-1)
    send_kv = jnp.take(cache_flat, send_slot, axis=0).reshape(inst_count, MIG, -1)
    send_len = jnp.take(lengths, send_slot).reshape(inst_count, MIG)
    got_kv, got_len = (
        lax.all_to_all(send_kv, "inst", split_axis=0, concat_axis=0, tiled=True),
        lax.all_to_all(send_len, "inst", split_axis=0, concat_axis=0, tiled=True),
    )
    kv_table = jnp.concatenate([cache_flat, got_kv.reshape(inst_count * MIG, -1)], axis=0)
    len_table = jnp.concatenate([lengths, got_len.reshape(-1)])
    row_index = jnp.where(is_local, my_from_slot, slot_count + remote_pos)
    moved = jnp.take(kv_table, row_index, axis=0).reshape(slot_count, heads_kv, depth, wide)
    moved_len = jnp.take(len_table, row_index).astype(jnp.int32)
    attended = attend(query_rows, pair_rows, moved, moved_len, heads_kv)
    partial_value = jnp.dot(attended, out_weight[0], preferred_element_type=jnp.float32)
    section_term = lax.psum_scatter(partial_value, "tp", scatter_dimension=1, tiled=True)
    own_section = lax.axis_index("section")
    running = section_term
    for hop_index in range(lax.axis_size("section") - 1):
        arrived = shifted(running, "section", 1)
        running = jnp.where(own_section == hop_index + 1, arrived + section_term, running)
    summed = hidden.astype(jnp.float32) + running
    return (summed[None].astype(jnp.bfloat16), moved[None], moved_len)


def solution(mesh):
    return jax.shard_map(
        body,
        mesh=mesh,
        in_specs=(
            P("inst", "tp"),
            P("section", "inst", "tp"),
            P("section", "inst", "tp"),
            P("section", "inst", "tp", None, None),
            P("inst"),
            P(),
            P("section", "tp", None),
        ),
        out_specs=(P("section", "inst", "tp"), P("section", "inst", "tp", None, None), P("inst")),
        check_vma=False,
    )
```

profile of v0, /device:TPU:1, one launch (start us, length us, event | category | flops | bytes accessed | tf_op | source)
XLA Modules:
  0.0 244.0 jit_solution(3010284869637749616)
XLA Ops:
  7.2 0.7 reshape.399
  7.9 0.2 reduce_window_sum.11
  8.1 0.1 select_reduce_fusion
  8.3 0.1 copy.22
  8.4 0.1 reshape.400
  8.5 1.3 gather_fusion
  9.9 0.1 copy.23
  10.0 0.7 copy.24
  10.6 4.8 %all-to-all-start = ((s32[4,1,2]{2,1,0:T(1,128)}), s32[4,1,2]{2,1,0:T(1,128)S(1)}, u32[]{:S(2)}, u32[]{:S(2)}) async-start(s32[4,1,2]{2,1,0:T(1,128)} %copy.24), calls=%async_computation | async-start | bytes 4096 | tf_op jit(solution)/shard_map/all_to_all | solution.py:84
  15.5 4.6 %copy.29 = bf16[2,8,512,256]{3,1,2,0:T(8,128)(2,1)S(1)} copy(bf16[2,8,512,256]{3,2,1,0:T(8,128)(2,1)} %bitcast.100) | data formatting | bytes 8388608
  20.1 1.8 fusion.30
  21.9 0.8 copy-done.2
  22.7 4.0 %gather_fusion.2 = bf16[8,65536]{1,0:T(8,128)(2,1)S(1)} fusion(bf16[16,65536]{1,0:T(8,128)(2,1)} %get-tuple-element.10, s32[1024]{0:T(1024)S(1)} %pad_clamp_fusion.1), kind=kCustom, calls=%fused_computation.2 | custom fusion | bytes 2097184 | tf_op jit(solution)/shard_map/jit(_take)/gather | solution.py:80
  26.7 2.2 gather_fusion.3
  28.9 2.7 %pad_maximum_fusion = bf16[8,131072]{1,0:T(8,128)(2,1)} fusion(bf16[8,65536]{1,0:T(8,128)(2,1)} %gather_fusion.3, bf16[8,65536]{1,0:T(8,128)(2,1)S(1)} %gather_fusion.2), kind=kLoop, calls=%fused_computation.15 | loop fusion | flops 4194304 | bytes 4194304
  31.6 2.9 %gather.28 = bf16[4,2,131072]{2,1,0:T(2,128)(2,1)S(1)} reshape(bf16[8,131072]{1,0:T(8,128)(2,1)} %pad_maximum_fusion) | data formatting | bytes 4194304 | tf_op jit(solution)/shard_map/jit(_take)/gather | solution.py:80
  34.5 0.1 copy.25
  34.6 3.2 %broadcast_select_fusion = bf16[4,2,131072]{2,1,0:T(2,128)(2,1)} fusion(bf16[4,2,131072]{2,1,0:T(2,128)(2,1)S(1)} %gather.28, pred[4,2]{1,0:T(4,128)(4,1)S(1)} %copy.25), kind=kLoop, calls=%fused_computation.10 | loop fusion | flops 1048576 | bytes 4194312 | tf_op jit(solution)/shard_map/jit(_take)/select_n | solution.py:80
  37.8 4.2 %all-to-all-start.1 = ((bf16[4,2,131072]{2,1,0:T(2,128)(2,1)}), bf16[4,2,131072]{2,1,0:T(2,128)(2,1)S(1)}, u32[]{:S(2)}, u32[]{:S(2)}) async-start(bf16[4,2,131072]{2,1,0:T(2,128)(2,1)} %broadcast_select_fusion), calls=%async_computation.1 | async-start | bytes 4194304 | tf_op jit(solution)/shard_map/all_to_all | solution.py:83
  42.0 0.2 reduce-scatter.2.cloned.1.call-start
  42.3 4.4 %constant_dynamic-update-slice_fusion.1 = bf16[24,131072]{1,0:T(8,128)(2,1)} fusion(bf16[16,131072]{1,0:T(8,128)(2,1)} %bitcast.96), kind=kLoop, calls=%fused_computation.38 | loop fusion | bytes 8388608
  46.7 0.2 convert_reduce_fusion
  46.9 0.1 fusion.16
  47.1 0.5 broadcast.426
  47.6 0.7 reduce.7
  48.4 0.7 gather_fusion.1
  49.2 17.0 %all-to-all-done.1 = bf16[4,2,131072]{2,1,0:T(2,128)(2,1)S(1)} async-done(((bf16[4,2,131072]{2,1,0:T(2,128)(2,1)}), bf16[4,2,131072]{2,1,0:T(2,128)(2,1)S(1)}, u32[]{:S(2)}, u32[]{:S(2)}) %all-to-all-start.1) | async-done | bytes 2097184 | tf_op jit(solution)/shard_map/all_to_all | solution.py:83
  66.2 2.1 reshape.402
  68.3 3.1 %constant_dynamic-update-slice_fusion = bf16[24,131072]{1,0:T(8,128)(2,1)} fusion(bf16[24,131072]{1,0:T(8,128)(2,1)} %constant_dynamic-update-slice_fusion.1, bf16[8,131072]{1,0:T(8,128)(2,1)} %reshape.402), kind=kLoop, calls=%fused_computation.37 | loop fusion | bytes 4194304 | tf_op jit(solution)/shard_map/concatenate | solution.py:86
  71.4 4.9 %fusion.29 = (bf16[24,65536]{1,0:T(8,128)(2,1)S(1)}, bf16[24,65536]{1,0:T(8,128)(2,1)}) fusion(bf16[24,131072]{1,0:T(8,128)(2,1)} %constant_dynamic-update-slice_fusion), kind=kLoop, calls=%fused_computation.92 | loop fusion | bytes 12582912 | tf_op jit(solution)/shard_map/jit(_take)/gather | solution.py:89
  76.3 7.3 %gather_fusion.4 = bf16[16,65536]{1,0:T(8,128)(2,1)} fusion(bf16[24,65536]{1,0:T(8,128)(2,1)} %get-tuple-element.9, s32[1024]{0:T(1024)S(1)} %pad_clamp_fusion), kind=kCustom, calls=%fused_computation.4 | custom fusion | bytes 4194368 | tf_op jit(solution)/shard_map/jit(_take)/gather | solution.py:89
  83.6 3.0 %constant_dynamic-update-slice_fusion.3 = bf16[16,131072]{1,0:T(8,128)(2,1)} fusion(bf16[16,65536]{1,0:T(8,128)(2,1)} %gather_fusion.4), kind=kLoop, calls=%fused_computation.40 | loop fusion | bytes 4194304
  86.6 3.3 %gather_fusion.5 = bf16[16,65536]{1,0:T(8,128)(2,1)} fusion(bf16[24,65536]{1,0:T(8,128)(2,1)S(1)} %get-tuple-element.8, s32[1024]{0:T(1024)S(1)} %pad_clamp_fusion), kind=kCustom, calls=%fused_computation.5 | custom fusion | bytes 4194368 | tf_op jit(solution)/shard_map/jit(_take)/gather | solution.py:89
  89.9 3.0 %constant_dynamic-update-slice_fusion.2 = bf16[16,131072]{1,0:T(8,128)(2,1)} fusion(bf16[16,131072]{1,0:T(8,128)(2,1)} %constant_dynamic-update-slice_fusion.3, bf16[16,65536]{1,0:T(8,128)(2,1)} %gather_fusion.5), kind=kLoop, calls=%fused_computation.39 | loop fusion | bytes 4194304
  92.9 3.3 %copy.30 = bf16[2,8,512,256]{3,2,1,0:T(8,128)(2,1)S(1)} copy(bf16[2,8,512,256]{3,1,2,0:T(8,128)(2,1)} %bitcast.99) | data formatting | bytes 8388608
  96.2 0.7 bitcast_select_fusion
  96.9 1.4 copy-done.1
  98.3 0.7 fusion.31
  99.1 0.2 fusion.9
  99.3 0.4 fusion.8
  99.8 0.2 slice-done.1
  100.0 2.0 fusion
  102.0 86.2 %reduce-scatter.2.cloned.1.call-done = f32[16,1024]{1,0:T(8,128)} async-done(((f32[16,8192]{1,0:T(8,128)}), f32[16,1024]{1,0:T(8,128)}) %reduce-scatter.2.cloned.1.call-update) | async-done | bytes 65552 | tf_op jit(solution)/shard_map/reduce_scatter | solution.py:93
  188.2 4.8 %collective-permute-start = (f32[16,1024]{1,0:T(8,128)}, f32[16,1024]{1,0:T(8,128)S(1)}, u32[]{:S(2)}, u32[]{:S(2)}) collective-permute-start(f32[16,1024]{1,0:T(8,128)} %reduce-scatter.2.cloned.1.call-done), channel_id=1, source_target_pairs={{0,8},{8,16},{16,24},{24,32},{32,40},{40,48},{48,56},{1,9},{9,17},... | collective-permute-start | bytes 196616 | tf_op jit(solution)/shard_map/ppermute | solution.py:14
  192.9 1.6 collective-permute-done
  194.6 0.8 add_select_fusion
  195.4 4.2 %collective-permute-start.1 = (f32[16,1024]{1,0:T(8,128)S(1)}, f32[16,1024]{1,0:T(8,128)S(1)}, u32[]{:S(2)}, u32[]{:S(2)}) collective-permute-start(f32[16,1024]{1,0:T(8,128)S(1)} %add_select_fusion), channel_id=1, source_target_pairs={{0,8},{8,16},{16,24},{24,32},{32,40},{40,48},{48,56},{1,9},{9,17},... | collective-permute-start | bytes 196616 | tf_op jit(solution)/shard_map/ppermute | solution.py:14
  199.6 1.3 collective-permute-done.1
  200.9 0.9 add_select_fusion.5
  201.7 4.3 %collective-permute-start.2 = (f32[16,1024]{1,0:T(8,128)S(1)}, f32[16,1024]{1,0:T(8,128)S(1)}, u32[]{:S(2)}, u32[]{:S(2)}) collective-permute-start(f32[16,1024]{1,0:T(8,128)S(1)} %add_select_fusion.5), channel_id=1, source_target_pairs={{0,8},{8,16},{16,24},{24,32},{32,40},{40,48},{48,56},{1,9},{9,17},... | collective-permute-start | bytes 196616 | tf_op jit(solution)/shard_map/ppermute | solution.py:14
  206.0 1.3 collective-permute-done.2
  207.3 0.9 add_select_fusion.4
  208.2 4.3 %collective-permute-start.3 = (f32[16,1024]{1,0:T(8,128)S(1)}, f32[16,1024]{1,0:T(8,128)S(1)}, u32[]{:S(2)}, u32[]{:S(2)}) collective-permute-start(f32[16,1024]{1,0:T(8,128)S(1)} %add_select_fusion.4), channel_id=1, source_target_pairs={{0,8},{8,16},{16,24},{24,32},{32,40},{40,48},{48,56},{1,9},{9,17},... | collective-permute-start | bytes 196616 | tf_op jit(solution)/shard_map/ppermute | solution.py:14
  212.5 1.3 collective-permute-done.3
  213.8 0.9 add_select_fusion.3
  214.6 4.3 %collective-permute-start.4 = (f32[16,1024]{1,0:T(8,128)S(1)}, f32[16,1024]{1,0:T(8,128)S(1)}, u32[]{:S(2)}, u32[]{:S(2)}) collective-permute-start(f32[16,1024]{1,0:T(8,128)S(1)} %add_select_fusion.3), channel_id=1, source_target_pairs={{0,8},{8,16},{16,24},{24,32},{32,40},{40,48},{48,56},{1,9},{9,17},... | collective-permute-start | bytes 196616 | tf_op jit(solution)/shard_map/ppermute | solution.py:14
  218.9 1.3 collective-permute-done.4
  220.2 0.9 add_select_fusion.2
  221.1 4.3 %collective-permute-start.5 = (f32[16,1024]{1,0:T(8,128)S(1)}, f32[16,1024]{1,0:T(8,128)S(1)}, u32[]{:S(2)}, u32[]{:S(2)}) collective-permute-start(f32[16,1024]{1,0:T(8,128)S(1)} %add_select_fusion.2), channel_id=1, source_target_pairs={{0,8},{8,16},{16,24},{24,32},{32,40},{40,48},{48,56},{1,9},{9,17},... | collective-permute-start | bytes 196616 | tf_op jit(solution)/shard_map/ppermute | solution.py:14
  225.4 1.3 collective-permute-done.5
  226.7 0.9 add_select_fusion.1
  227.5 4.3 %collective-permute-start.6 = (f32[16,1024]{1,0:T(8,128)S(1)}, f32[16,1024]{1,0:T(8,128)S(1)}, u32[]{:S(2)}, u32[]{:S(2)}) collective-permute-start(f32[16,1024]{1,0:T(8,128)S(1)} %add_select_fusion.1), channel_id=1, source_target_pairs={{0,8},{8,16},{16,24},{24,32},{32,40},{40,48},{48,56},{1,9},{9,17},... | collective-permute-start | bytes 196616 | tf_op jit(solution)/shard_map/ppermute | solution.py:14
  231.8 4.7 %bitcast_select_fusion.1 = bf16[1,16,1,512,256]{4,3,2,1,0:T(8,128)(2,1)} fusion(bf16[1,16,1,512,256]{4,3,1,2,0:T(8,128)(2,1)} %bitcast.94, pred[16]{0:T(512)(128)(4,1)S(1)} %get-tuple-element.4), kind=kLoop, calls=%fused_computation.9 | loop fusion | flops 2097152 | bytes 8388624 | tf_op jit(solution)/shard_map/jit(_take)/select_n | solution.py:89
  236.5 0.6 fusion.12
  (39 shorter events, 0.5 us)
Async XLA Ops:
  10.6 27.1 %all-to-all-start = ((s32[4,1,2]{2,1,0:T(1,128)}), s32[4,1,2]{2,1,0:T(1,128)S(1)}, u32[]{:S(2)}, u32[]{:S(2)}) async-start(s32[4,1,2]{2,1,0:T(1,128)} %copy.24), calls=%async_computation | async-start | bytes 4096 | tf_op jit(solution)/shard_map/all_to_all | solution.py:84
  20.1 2.6 %copy-start.2 = (bf16[2,8,512,256]{3,1,2,0:T(8,128)(2,1)}, bf16[2,8,512,256]{3,1,2,0:T(8,128)(2,1)S(1)}, u32[]{:S(2)}) copy-start(bf16[2,8,512,256]{3,1,2,0:T(8,128)(2,1)S(1)} %copy.29) | copy-start | bytes 12582916
  37.8 28.4 %all-to-all-start.1 = ((bf16[4,2,131072]{2,1,0:T(2,128)(2,1)}), bf16[4,2,131072]{2,1,0:T(2,128)(2,1)S(1)}, u32[]{:S(2)}, u32[]{:S(2)}) async-start(bf16[4,2,131072]{2,1,0:T(2,128)(2,1)} %broadcast_select_fusion), calls=%async_computation.1 | async-start | bytes 4194304 | tf_op jit(solution)/shard_map/all_to_all | solution.py:83
  42.0 4.6 %copy-start.5 = (bf16[1,16,512]{2,1,0:T(8,128)(2,1)S(1)}, bf16[1,16,512]{2,1,0:T(8,128)(2,1)}, u32[]{:S(2)}) copy-start(bf16[1,16,512]{2,1,0:T(8,128)(2,1)} %param.8) | copy-start | bytes 49156
  42.0 4.9 %copy-start.6 = (bf16[1,16,256]{2,1,0:T(8,128)(2,1)S(1)}, bf16[1,16,256]{2,1,0:T(8,128)(2,1)}, u32[]{:S(2)}) copy-start(bf16[1,16,256]{2,1,0:T(8,128)(2,1)} %param.9) | copy-start | bytes 24580
  42.0 6.3 %copy-start = (s32[16]{0:T(128)S(1)}, s32[16]{0:T(128)}, u32[]{:S(2)}) copy-start(s32[16]{0:T(128)} %param.11) | copy-start | bytes 196
  42.0 146.1 %reduce-scatter.2.cloned.1.call-start = ((), (), s32[]{:S(2)}) async-start(), calls=%async_computation.3 | async-start | bytes 589824 | tf_op jit(solution)/shard_map/reduce_scatter | solution.py:93
  49.1 22.3 %copy-start.7 = (s32[16]{0:T(128)}, s32[16]{0:T(128)S(1)}, u32[]{:S(2)}) copy-start(s32[16]{0:T(128)S(1)} %get-tuple-element.3) | copy-start | bytes 196
  92.9 6.8 %slice-start = ((s8[8388608]{0:T(1024)(128)(4,1)}), s8[4194304]{0:T(1024)(128)(4,1)S(1)}, s32[]{:S(2)}) async-start(s8[8388608]{0:T(1024)(128)(4,1)} %bitcast.97), calls=%async_computation.4 | async-start | bytes 8388608
  96.2 2.1 copy-start.1
  96.2 3.7 %slice-start.1 = ((s8[8388608]{0:T(1024)(128)(4,1)}), s8[4194304]{0:T(1024)(128)(4,1)S(1)}, s32[]{:S(2)}) async-start(s8[8388608]{0:T(1024)(128)(4,1)} %bitcast.97), calls=%async_computation.5 | async-start | bytes 8388608
  188.2 6.4 %collective-permute-start = (f32[16,1024]{1,0:T(8,128)}, f32[16,1024]{1,0:T(8,128)S(1)}, u32[]{:S(2)}, u32[]{:S(2)}) collective-permute-start(f32[16,1024]{1,0:T(8,128)} %reduce-scatter.2.cloned.1.call-done), channel_id=1, source_target_pairs={{0,8},{8,16},{16,24},{24,32},{32,40},{40,48},{48,56},{1,9},{9,17},... | collective-permute-start | bytes 196616 | tf_op jit(solution)/shard_map/ppermute | solution.py:14
  195.4 5.5 %collective-permute-start.1 = (f32[16,1024]{1,0:T(8,128)S(1)}, f32[16,1024]{1,0:T(8,128)S(1)}, u32[]{:S(2)}, u32[]{:S(2)}) collective-permute-start(f32[16,1024]{1,0:T(8,128)S(1)} %add_select_fusion), channel_id=1, source_target_pairs={{0,8},{8,16},{16,24},{24,32},{32,40},{40,48},{48,56},{1,9},{9,17},... | collective-permute-start | bytes 196616 | tf_op jit(solution)/shard_map/ppermute | solution.py:14
  201.7 5.6 %collective-permute-start.2 = (f32[16,1024]{1,0:T(8,128)S(1)}, f32[16,1024]{1,0:T(8,128)S(1)}, u32[]{:S(2)}, u32[]{:S(2)}) collective-permute-start(f32[16,1024]{1,0:T(8,128)S(1)} %add_select_fusion.5), channel_id=1, source_target_pairs={{0,8},{8,16},{16,24},{24,32},{32,40},{40,48},{48,56},{1,9},{9,17},... | collective-permute-start | bytes 196616 | tf_op jit(solution)/shard_map/ppermute | solution.py:14
  208.2 5.6 %collective-permute-start.3 = (f32[16,1024]{1,0:T(8,128)S(1)}, f32[16,1024]{1,0:T(8,128)S(1)}, u32[]{:S(2)}, u32[]{:S(2)}) collective-permute-start(f32[16,1024]{1,0:T(8,128)S(1)} %add_select_fusion.4), channel_id=1, source_target_pairs={{0,8},{8,16},{16,24},{24,32},{32,40},{40,48},{48,56},{1,9},{9,17},... | collective-permute-start | bytes 196616 | tf_op jit(solution)/shard_map/ppermute | solution.py:14
  214.6 5.6 %collective-permute-start.4 = (f32[16,1024]{1,0:T(8,128)S(1)}, f32[16,1024]{1,0:T(8,128)S(1)}, u32[]{:S(2)}, u32[]{:S(2)}) collective-permute-start(f32[16,1024]{1,0:T(8,128)S(1)} %add_select_fusion.3), channel_id=1, source_target_pairs={{0,8},{8,16},{16,24},{24,32},{32,40},{40,48},{48,56},{1,9},{9,17},... | collective-permute-start | bytes 196616 | tf_op jit(solution)/shard_map/ppermute | solution.py:14
  221.1 5.6 %collective-permute-start.5 = (f32[16,1024]{1,0:T(8,128)S(1)}, f32[16,1024]{1,0:T(8,128)S(1)}, u32[]{:S(2)}, u32[]{:S(2)}) collective-permute-start(f32[16,1024]{1,0:T(8,128)S(1)} %add_select_fusion.2), channel_id=1, source_target_pairs={{0,8},{8,16},{16,24},{24,32},{32,40},{40,48},{48,56},{1,9},{9,17},... | collective-permute-start | bytes 196616 | tf_op jit(solution)/shard_map/ppermute | solution.py:14
  227.5 9.0 %collective-permute-start.6 = (f32[16,1024]{1,0:T(8,128)S(1)}, f32[16,1024]{1,0:T(8,128)S(1)}, u32[]{:S(2)}, u32[]{:S(2)}) collective-permute-start(f32[16,1024]{1,0:T(8,128)S(1)} %add_select_fusion.1), channel_id=1, source_target_pairs={{0,8},{8,16},{16,24},{24,32},{32,40},{40,48},{48,56},{1,9},{9,17},... | collective-permute-start | bytes 196616 | tf_op jit(solution)/shard_map/ppermute | solution.py:14
  231.8 4.7 %copy-start.3 = (f32[16,1024]{1,0:T(8,128)S(1)}, f32[16,1024]{1,0:T(8,128)}, u32[]{:S(2)}) copy-start(f32[16,1024]{1,0:T(8,128)} %reduce-scatter.2.cloned.1.call-done) | copy-start | bytes 196612
  231.8 4.7 %copy-start.4 = (bf16[16,1024]{1,0:T(8,128)(2,1)S(1)}, bf16[16,1024]{1,0:T(8,128)(2,1)}, u32[]{:S(2)}) copy-start(bf16[16,1024]{1,0:T(8,128)(2,1)} %param.7) | copy-start | bytes 98308
Sparse Core Ops, SparseCore 0:
  102.1 86.0 reduce-scatter.1
where the time goes:
time: 245 us; the launch traced here: 244 us
  waiting for transfers between devices  111 us (45%)
  local copies, waits for them, and re-layouts  56.8 us (23%)
  starting transfers between devices  39.6 us (16%)
  other arithmetic  18.7 us (8%)
  between operations  14.3 us (6%)
  matrix products  3.3 us (1%)
    reduce_scatter x1, waiting for transfers between devices, body(): lax.psum_scatter(partial_value, 'tp', scatter_dimension=1, tiled=True)  86.2 us
    ppermute x7, starting transfers between devices, shifted(): lax.ppermute(value, axis, [(source, source + steps) for source in range(f...  30.3 us
    unnamed x25, local copies, waits for them, and re-layouts  20.9 us
    all_to_all x1, waiting for transfers between devices, body(): lax.all_to_all(send_kv, 'inst', split_axis=0, concat_axis=0, tiled=True)  17 us
    gather x3, local copies, waits for them, and re-layouts, body(): jnp.take(kv_table, row_index, axis=0)  15.4 us
    gather x4, local copies, waits for them, and re-layouts, body(): jnp.take(cache_flat, send_slot, axis=0).reshape(inst_count, MIG, -1)  10.8 us
    ppermute x7, waiting for transfers between devices, shifted(): lax.ppermute(value, axis, [(source, source + steps) for source in range(f...  8.15 us
    select_n x2, other arithmetic, body(): jnp.take(kv_table, row_index, axis=0)  5.37 us
  transfers between devices with their start and end apart: 10, of which 8 were waited for; matrix products, arithmetic and copies ran while one was open for 14% of the time, Pallas kernels for 0%

commit v1 on v0

v1 whole, which is shorter than its diff:
```python
import functools
import math

import jax
import jax.numpy as jnp
from jax import lax
from jax.experimental import pallas as pl
from jax.experimental.pallas import tpu as pltpu
from jax.sharding import PartitionSpec as P

MESH = pl.DeviceIdType.MESH
BF = jnp.bfloat16
F32 = jnp.float32
I32 = jnp.int32

INST = 4
TP = 8
SECTIONS = 8
SLOTS = 16
MIG = 2
GROUP = 4
HD = 128
CTX = 512
MODEL = 8192
COLS = MODEL // TP
FIRST = 256
SHIFTS = (1, 2, 3)
MOVES = len(SHIFTS) * MIG
ORDER = (3, 5, 1, 7, 4, 2, 6)
INV_ROOT = 1.0 / math.sqrt(HD)

AT_DEST = 0
AT_LEN = 8
AT_SLOT = 16
AT_POS = 32
INFO = 48


def wrap(value, count):
    return lax.rem(value + count, count)


def attend_slot(query, keys, values, length, first_len=None):
    rows = query.astype(BF)
    parts = [
        lax.dot_general(rows, block, (((1,), (1,)), ((), ())), preferred_element_type=F32) for block in keys
    ]
    scores = (parts[0] if len(parts) == 1 else jnp.concatenate(parts, axis=1)) * INV_ROOT
    new_key, new_value = query[4:5, :], query[5:6, :]
    new_score = jnp.sum(query * new_key, axis=1, keepdims=True) * INV_ROOT
    place = lax.broadcasted_iota(I32, scores.shape, 1)
    scores = jnp.where(place < length, scores, -jnp.inf)
    top = jnp.maximum(jnp.max(scores, axis=1, keepdims=True), new_score)
    expo = jnp.exp(scores - top)
    new_expo = jnp.exp(new_score - top)
    total = jnp.sum(expo, axis=1, keepdims=True) + new_expo
    probs = (expo / total).astype(BF)
    new_prob = (new_expo / total).astype(BF).astype(F32)
    result = new_prob * new_value
    start = 0
    for block in values:
        stop = start + block.shape[0]
        result = result + jnp.dot(probs[:, start:stop], block, preferred_element_type=F32)
        start = stop
    return result


def gather_kernel(anchor, lengths, q_ref, new_ref, kv, q_slots, s1, s2, s3, a1, a2, a3, b1, b2, b3, info, sems):
    me = lax.axis_index("inst")
    first, second = (a1, a2, a3), (b1, b2, b3)
    copies = []
    for at, shift in enumerate(SHIFTS):
        dest = wrap(me + shift, INST)
        count = jnp.int32(0)
        picked = [jnp.int32(0)] * MIG
        for slot in range(SLOTS):
            source = anchor[dest * SLOTS + slot]
            hit = lax.shift_right_logical(source, 4) == me
            for rank in range(MIG):
                picked[rank] = jnp.where(hit & (count == rank), source & (SLOTS - 1), picked[rank])
            count = count + hit.astype(I32)
        for rank in range(MIG):
            one = at * MIG + rank
            info[AT_LEN + one] = lengths[picked[rank]]
            for part, (refs, begin, size) in enumerate(((first, 0, FIRST), (second, FIRST, CTX - FIRST))):
                copy = pltpu.make_async_copy(
                    kv.at[0, picked[rank], 0, pl.ds(begin, size)], refs[at].at[rank], sems.at[part, one]
                )
                copy.start()
                copies.append(copy)
    queries = q_ref[0].astype(F32)
    pairs = new_ref[0].astype(F32)
    for head in range(GROUP):
        q_slots[:, head, :] = queries[:, head * HD : (head + 1) * HD]
    q_slots[:, 4, :] = pairs[:, :HD]
    q_slots[:, 5, :] = pairs[:, HD:]
    q_slots[:, 6, :] = jnp.zeros((SLOTS, HD), F32)
    q_slots[:, 7, :] = jnp.zeros((SLOTS, HD), F32)
    counts = [jnp.int32(0)] * len(SHIFTS)
    found = [jnp.int32(0)] * MOVES
    for slot in range(SLOTS):
        source = anchor[me * SLOTS + slot]
        owner = lax.shift_right_logical(source, 4)
        position = jnp.int32(-1)
        for at, shift in enumerate(SHIFTS):
            hit = owner == wrap(me - shift, INST)
            position = jnp.where(hit, at * MIG + counts[at], position)
            for rank in range(MIG):
                one = at * MIG + rank
                found[one] = jnp.where(hit & (counts[at] == rank), slot, found[one])
            counts[at] = counts[at] + hit.astype(I32)
        info[AT_SLOT + slot] = source & (SLOTS - 1)
        info[AT_POS + slot] = position
    for at, out in enumerate((s1, s2, s3)):
        for rank in range(MIG):
            info[AT_DEST + at * MIG + rank] = found[at * MIG + rank]
        out[...] = jnp.concatenate([q_slots[found[at * MIG + rank]] for rank in range(MIG)], axis=0).astype(BF)
    for spare in (AT_DEST + 6, AT_DEST + 7, AT_LEN + 6, AT_LEN + 7):
        info[spare] = jnp.int32(0)
    for copy in copies:
        copy.wait()


def local_kernel(info, lengths, q_slots, kv, moved, attended, cache, result, read_sems, write_sems):
    def is_local(slot):
        return info[AT_POS + slot] < 0

    def read(slot):
        return pltpu.make_async_copy(kv.at[0, info[AT_SLOT + slot], 0], cache.at[slot], read_sems.at[slot])

    def write(slot):
        return pltpu.make_async_copy(cache.at[slot], moved.at[0, slot, 0], write_sems.at[slot])

    for slot in range(SLOTS):
        pl.when(is_local(slot))(lambda slot=slot: read(slot).start())
    result[...] = jnp.zeros_like(result)
    for slot in range(SLOTS):

        @pl.when(is_local(slot))
        def _(slot=slot):
            read(slot).wait()
            write(slot).start()
            length = lengths[info[AT_SLOT + slot]]
            result[slot] = attend_slot(
                q_slots[slot], [cache[slot, :, :HD]], [cache[slot, :, HD:]], length
            )

    attended[...] = jnp.concatenate([result[:, head, :] for head in range(GROUP)], axis=1).astype(BF)
    for slot in range(SLOTS):
        pl.when(is_local(slot))(lambda slot=slot: write(slot).wait())


def chain_kernel(
    info, lengths, q1, q2, q3, a1, a2, a3, b1, b2, b3, attended, hidden, weight,
    c1, c2, c3, out, moved_len,
    w_blocks, send_l, recv_l, send_m, recv_m, delta_l, part_l, delta_m, part_m,
    back, back_in, tile, tile_in, rows_m, rows, acc_m,
    w_sems, back_sems, tile_sems, bulk_sems, l_sems, m_sems, pl_sems, pm_sems,
):
    inst, section, tp = (lax.axis_index(name) for name in ("inst", "section", "tp"))
    queries, first, second, arrived = (q1, q2, q3), (a1, a2, a3), (b1, b2, b3), (c1, c2, c3)

    def on_inst(shift):
        return {"inst": wrap(inst + shift, INST)}

    def on_tp(distance):
        return {"tp": wrap(tp + distance, TP)}

    def remote(source, target, sems, at, device):
        return pltpu.make_async_remote_copy(
            src_ref=source, dst_ref=target, send_sem=sems.at[0, at], recv_sem=sems.at[1, at],
            device_id=device, device_id_type=MESH,
        )

    barrier = pltpu.get_barrier_semaphore()
    for shift in SHIFTS:
        pl.semaphore_signal(barrier, inc=1, device_id=on_inst(shift), device_id_type=MESH)
    for distance in ORDER:
        pl.semaphore_signal(barrier, inc=1, device_id=on_tp(distance), device_id_type=MESH)
    for distance in range(1, SECTIONS):

        @pl.when(section >= distance)
        def _(distance=distance):
            pl.semaphore_signal(barrier, inc=1, device_id={"section": section - distance}, device_id_type=MESH)

    loads = {}
    for distance in ORDER + (0,):
        columns = pl.ds(pl.multiple_of(wrap(tp + distance, TP) * COLS, COLS), COLS)
        loads[distance] = pltpu.make_async_copy(
            weight.at[0, :, columns], w_blocks.at[distance], w_sems.at[distance]
        )
        loads[distance].start()

    for at in range(len(SHIFTS)):
        both = queries[at][...].astype(F32)
        results = []
        for rank in range(MIG):
            results.append(
                attend_slot(
                    both[rank * 8 : rank * 8 + 8, :],
                    [first[at][rank, :, :HD], second[at][rank, :, :HD]],
                    [first[at][rank, :, HD:], second[at][rank, :, HD:]],
                    info[AT_LEN + at * MIG + rank],
                )
            )
        back[at] = jnp.concatenate(results, axis=0).astype(BF)
    lane = lax.broadcasted_iota(I32, (8, 128), 1)
    for at in range(len(SHIFTS)):
        filled = jnp.zeros((8, 128), I32)
        for rank in range(MIG):
            filled = jnp.where(lane == rank, info[AT_LEN + at * MIG + rank], filled)
        tile[at] = filled

    pl.semaphore_wait(barrier, len(SHIFTS) + TP - 1 + SECTIONS - 1 - section)

    back_copies, tile_copies, bulk_copies = [], [], []
    for at, shift in enumerate(SHIFTS):
        back_copies.append(remote(back.at[at], back_in.at[at], back_sems, at, on_inst(shift)))
        tile_copies.append(remote(tile.at[at], tile_in.at[at], tile_sems, at, on_inst(shift)))
        bulk_copies.append(remote(second[at], arrived[at], bulk_sems, at, on_inst(shift)))
    for copy in back_copies + tile_copies:
        copy.start()
    for copy in (bulk_copies[1], bulk_copies[0], bulk_copies[2]):
        copy.start()

    stay = attended[...]
    stay_copies = {}
    own_l = None
    for distance in ORDER + (0,):
        loads[distance].wait()
        share = jnp.dot(stay, w_blocks[distance], preferred_element_type=F32)
        if distance == 0:
            own_l = share
        else:
            send_l[distance] = share.astype(BF)
            copy = remote(send_l.at[distance], recv_l.at[distance], l_sems, distance, on_tp(distance))
            copy.start()
            stay_copies[distance] = copy

    for copy in back_copies:
        copy.wait_recv()
    for at in range(len(SHIFTS)):
        both = back_in[at].astype(F32)
        for rank in range(MIG):
            rows_m[at * MIG + rank] = both[rank * 8 : rank * 8 + 8, :]
    rows_m[6] = jnp.zeros((8, HD), F32)
    rows_m[7] = jnp.zeros((8, HD), F32)
    come = jnp.concatenate([rows_m[:, head, :] for head in range(GROUP)], axis=1).astype(BF)
    half = COLS // 2
    come_copies = {}
    own_m = None
    for distance in ORDER + (0,):
        share = jnp.dot(come, w_blocks[distance], preferred_element_type=F32)
        share = jnp.concatenate([share[:, :half], share[:, half:]], axis=0)
        if distance == 0:
            own_m = share
        else:
            send_m[distance] = share.astype(BF)
            copy = remote(send_m.at[distance], recv_m.at[distance], m_sems, distance, on_tp(distance))
            copy.start()
            come_copies[distance] = copy

    def later(group, source, target, sems, do):
        for distance in range(1, SECTIONS):

            @pl.when(section + distance < SECTIONS)
            def _(distance=distance):
                do(remote(source, target.at[distance], sems, distance, {"section": section + distance}))

    def start(copy):
        copy.start()

    def sent(copy):
        copy.wait_send()

    total = own_l
    for distance in ORDER:
        stay_copies[distance].wait_recv()
        total = total + recv_l[distance].astype(F32)
    delta_l[...] = total.astype(BF)
    later("stay", delta_l, part_l, pl_sems, start)
    rows[...] = hidden[...].astype(F32) + total
    total = own_m
    for distance in ORDER:
        come_copies[distance].wait_recv()
        total = total + recv_m[distance].astype(F32)
    delta_m[...] = total.astype(BF)
    later("come", delta_m, part_m, pm_sems, start)
    acc_m[...] = total

    for copy in tile_copies:
        copy.wait_recv()
    lens = jnp.zeros((8, 128), I32)
    for slot in range(SLOTS):
        lens = jnp.where(lane == slot, lengths[info[AT_SLOT + slot]], lens)
    for at in range(len(SHIFTS)):
        for rank in range(MIG):
            value = jnp.sum(jnp.where(lane == rank, tile_in[at], 0), axis=1, keepdims=True)
            lens = jnp.where(lane == info[AT_DEST + at * MIG + rank], value, lens)
    moved_len[...] = lens

    for distance in range(1, SECTIONS):

        @pl.when(section >= distance)
        def _(distance=distance):
            remote(delta_l, part_l.at[distance], pl_sems, distance, {"section": section}).wait_recv()
            rows[...] += part_l[distance].astype(F32)

    for distance in range(1, SECTIONS):

        @pl.when(section >= distance)
        def _(distance=distance):
            remote(delta_m, part_m.at[distance], pm_sems, distance, {"section": section}).wait_recv()
            acc_m[...] += part_m[distance].astype(F32)

    low, high = acc_m.at[pl.ds(0, 8)], acc_m.at[pl.ds(8, 8)]
    for slot in range(SLOTS):
        position = info[AT_POS + slot]
        place = jnp.maximum(position, 0)
        for part, ref in enumerate((low, high)):
            extra = jnp.where(position >= 0, ref[pl.ds(place, 1), :], 0.0)
            rows[slot : slot + 1, part * half : (part + 1) * half] += extra
    out[...] = rows[...].astype(BF)

    later("stay", delta_l, part_l, pl_sems, sent)
    later("come", delta_m, part_m, pm_sems, sent)
    for copy in list(stay_copies.values()) + list(come_copies.values()) + back_copies + tile_copies:
        copy.wait_send()
    for copy in bulk_copies:
        copy.wait()


def place_kernel(info, a1, a2, a3, c1, c2, c3, out_rows, lens, moved_in, moved, out, moved_len, scalars, sems, more):
    del moved_in
    copies = [
        pltpu.make_async_copy(out_rows, out.at[0], more.at[0]),
        pltpu.make_async_copy(lens, scalars, more.at[1]),
    ]
    for at, (early, late) in enumerate(zip((a1, a2, a3), (c1, c2, c3))):
        for rank in range(MIG):
            one = at * MIG + rank
            target = moved.at[0, info[AT_DEST + one], 0]
            copies.append(
                pltpu.make_async_copy(early.at[rank], target.at[pl.ds(0, FIRST)], sems.at[0, one])
            )
            copies.append(
                pltpu.make_async_copy(late.at[rank], target.at[pl.ds(FIRST, CTX - FIRST)], sems.at[1, one])
            )
    for copy in copies:
        copy.start()
    copies[1].wait()
    for slot in range(SLOTS):
        moved_len[slot] = scalars[0, slot]
    for copy in copies[:1] + copies[2:]:
        copy.wait()


def specs(*spaces):
    return [pl.BlockSpec(memory_space=space) for space in spaces]


def body(hidden, queries, new_kv, kv_cache, lengths, anchor, out_weight):
    vmem, smem, hbm = pltpu.VMEM, pltpu.SMEM, pltpu.HBM
    dma = pltpu.SemaphoreType.DMA
    rest = CTX - FIRST
    early = [vmem((MIG, FIRST, 2 * HD), BF)] * 3
    late = [vmem((MIG, rest, 2 * HD), BF)] * 3
    gathered = pl.pallas_call(
        gather_kernel,
        out_shape=[vmem((SLOTS, 8, HD), F32)] + [vmem((16, HD), BF)] * 3 + early + late
        + [jax.ShapeDtypeStruct((INFO,), I32)],
        in_specs=specs(smem, smem, vmem, vmem, hbm),
        out_specs=specs(*[vmem] * 10, smem),
        scratch_shapes=[dma((2, MOVES))],
        compiler_params=pltpu.CompilerParams(vmem_limit_bytes=8 << 20),
        name="gather",
    )(anchor, lengths, queries, new_kv, kv_cache)
    q_slots, asked, first, second, info = gathered[0], gathered[1:4], gathered[4:7], gathered[7:10], gathered[10]

    def permute(value, shift):
        return lax.ppermute(value, "inst", [(i, (i + shift) % INST) for i in range(INST)])

    asked = [permute(value, -shift) for value, shift in zip(asked, SHIFTS)]
    first_in = [permute(value, shift) for value, shift in zip(first, SHIFTS)]
    moved, attended = pl.pallas_call(
        local_kernel,
        out_shape=[jax.ShapeDtypeStruct(kv_cache.shape, BF), vmem((SLOTS, GROUP * HD), BF)],
        in_specs=specs(smem, smem, vmem, hbm),
        out_specs=specs(hbm, vmem),
        scratch_shapes=[
            vmem((SLOTS, CTX, 2 * HD), BF), vmem((SLOTS, 8, HD), F32), dma((SLOTS,)), dma((SLOTS,)),
        ],
        compiler_params=pltpu.CompilerParams(vmem_limit_bytes=12 << 20),
        name="local",
    )(info, lengths, q_slots, kv_cache)
    arrived = pl.pallas_call(
        chain_kernel,
        out_shape=late + [vmem((SLOTS, COLS), BF), vmem((8, 128), I32)],
        in_specs=specs(smem, smem, *[vmem] * 11, hbm),
        out_specs=specs(*[vmem] * 5),
        scratch_shapes=[
            vmem((TP, GROUP * HD, COLS), BF),
            vmem((TP, 16, COLS), BF), vmem((TP, 16, COLS), BF),
            vmem((TP, 16, COLS // 2), BF), vmem((TP, 16, COLS // 2), BF),
            vmem((16, COLS), BF), vmem((SECTIONS, 16, COLS), BF),
            vmem((16, COLS // 2), BF), vmem((SECTIONS, 16, COLS // 2), BF),
            vmem((3, 16, HD), BF), vmem((3, 16, HD), BF),
            vmem((3, 8, 128), I32), vmem((3, 8, 128), I32),
            vmem((8, 8, HD), F32), vmem((SLOTS, COLS), F32), vmem((16, COLS // 2), F32),
            dma((TP,)), dma((2, 3)), dma((2, 3)), dma((2, 3)),
            dma((2, TP)), dma((2, TP)), dma((2, SECTIONS)), dma((2, SECTIONS)),
        ],
        compiler_params=pltpu.CompilerParams(
            collective_id=0, has_side_effects=True, vmem_limit_bytes=24 << 20
        ),
        name="chain",
    )(info, lengths, *asked, *first, *second, attended, hidden, out_weight)
    second_in, out_rows, lens = arrived[:3], arrived[3], arrived[4]
    moved, out, moved_len = pl.pallas_call(
        place_kernel,
        out_shape=[
            jax.ShapeDtypeStruct(kv_cache.shape, BF),
            jax.ShapeDtypeStruct((1, SLOTS, COLS), BF),
            jax.ShapeDtypeStruct((SLOTS,), I32),
        ],
        in_specs=specs(smem, *[vmem] * 8, hbm),
        out_specs=specs(hbm, hbm, smem),
        scratch_shapes=[pltpu.SMEM((8, 128), I32), dma((2, MOVES)), dma((2,))],
        input_output_aliases={9: 0},
        compiler_params=pltpu.CompilerParams(vmem_limit_bytes=8 << 20),
        name="place",
    )(info, *first_in, *second_in, out_rows, lens, moved)
    return out, moved, moved_len


def solution(mesh):
    return jax.shard_map(
        body,
        mesh=mesh,
        in_specs=(
            P("inst", "tp"),
            P("section", "inst", "tp"),
            P("section", "inst", "tp"),
            P("section", "inst", "tp", None, None),
            P("inst"),
            P(),
            P("section", "tp", None),
        ),
        out_specs=(P("section", "inst", "tp"), P("section", "inst", "tp", None, None), P("inst")),
        check_vma=False,
    )
```

time: 245 us -> 65.7 us (0.27)
  the two profiles are of different devices: /device:TPU:1 before, /device:TPU:103 now
where the time goes in v1:
time: 65.7 us; the launch traced here: 64.4 us
  Pallas kernels  39.6 us (60%)
  waiting for transfers between devices  9.48 us (14%)
  local copies, waits for them, and re-layouts  8.29 us (13%)
  starting transfers between devices  6.29 us (10%)
  between operations  0.73 us (1%)
    pallas_call x1, Pallas kernels, body(): pl.pallas_call(chain_kernel, out_shape=late + [vmem((SLOTS, COLS), BF), v...  27.7 us
    ppermute x6, waiting for transfers between devices, permute(): lax.ppermute(value, 'inst', [(i, (i + shift) % INST) for i in range(INST)])  9.48 us
    unnamed x18, local copies, waits for them, and re-layouts  8.29 us
    ppermute x6, starting transfers between devices, permute(): lax.ppermute(value, 'inst', [(i, (i + shift) % INST) for i in range(INST)])  6.29 us
    pallas_call x1, Pallas kernels, body(): pl.pallas_call(local_kernel, out_shape=[jax.ShapeDtypeStruct(kv_cache.sha...  5.86 us
    pallas_call x1, Pallas kernels, body(): pl.pallas_call(gather_kernel, out_shape=[vmem((SLOTS, 8, HD), F32)] + [vm...  3.7 us
    pallas_call x1, Pallas kernels, body(): pl.pallas_call(place_kernel, out_shape=[jax.ShapeDtypeStruct(kv_cache.sha...  2.32 us
  transfers between devices with their start and end apart: 6, of which 1 were waited for; matrix products, arithmetic and copies ran while one was open for 0% of the time, Pallas kernels for 52%

profile of v1, /device:TPU:103, one launch (start us, length us, event | category | flops | bytes accessed | tf_op | source)
XLA Modules:
  0.0 64.4 jit_solution(12609402300094751294)
XLA Ops:
  0.6 0.0 copy-start
  0.6 2.2 %copy-done = bf16[1,16,1,512,256]{4,3,2,1,0:T(8,128)(2,1)S(1)} copy-done((bf16[1,16,1,512,256]{4,3,2,1,0:T(8,128)(2,1)S(1)}, bf16[1,16,1,512,256]{4,3,2,1,0:T(8,128)(2,1)}, u32[]{:S(2)}) %copy-start) | copy-done | bytes 4194328
  2.8 0.0 copy-start.4
  2.8 0.7 %copy-done.4 = bf16[1,16,512]{2,1,0:T(8,128)(2,1)S(1)} copy-done((bf16[1,16,512]{2,1,0:T(8,128)(2,1)S(1)}, bf16[1,16,512]{2,1,0:T(8,128)(2,1)}, u32[]{:S(2)}) %copy-start.4) | copy-done | bytes 16408
  3.5 0.0 copy-start.5
  3.5 0.7 %copy-done.5 = bf16[1,16,256]{2,1,0:T(8,128)(2,1)S(1)} copy-done((bf16[1,16,256]{2,1,0:T(8,128)(2,1)S(1)}, bf16[1,16,256]{2,1,0:T(8,128)(2,1)}, u32[]{:S(2)}) %copy-start.5) | copy-done | bytes 8216
  4.2 0.0 copy-start.6
  4.2 0.7 %copy-done.6 = s32[16]{0:T(128)S(1)} copy-done((s32[16]{0:T(128)S(1)}, s32[16]{0:T(128)}, u32[]{:S(2)}) %copy-start.6) | copy-done | bytes 88
  4.9 0.0 copy-start.8
  4.9 0.7 %copy-done.8 = s32[64]{0:T(128)S(1)} copy-done((s32[64]{0:T(128)S(1)}, s32[64]{0:T(128)}, u32[]{:S(2)}) %copy-start.8) | copy-done | bytes 280
  5.5 0.0 copy-start.1
  5.5 0.0 copy-start.7
  5.6 0.0 copy-start.3
  5.6 3.7 %gather.1 = (f32[16,8,128]{2,1,0:T(8,128)S(1)}, bf16[16,128]{1,0:T(8,128)(2,1)S(1)}, bf16[16,128]{1,0:T(8,128)(2,1)S(1)}, bf16[16,128]{1,0:T(8,128)(2,1)S(1)}, b...) custom-call(s32[64]{0:T(128)S(1)} %copy-done.8, ...), custom_call_target="tpu_custom_call" | custom-call | tf_op jit(solution)/shard_map/gather/pallas_call | solution.py:368
  9.3 0.3 collective-permute-start
  9.5 2.1 %collective-permute-start.1 = (bf16[2,256,256]{2,1,0:T(8,128)(2,1)S(1)}, bf16[2,256,256]{2,1,0:T(8,128)(2,1)S(1)}, u32[]{:S(2)}, u32[]{:S(2)}) collective-permute-start(bf16[2,256,256]{2,1,0:T(8,128)(2,1)S(1)} %get-tuple-element.26.a2), channel_id=1, source_target_pairs={{0,128},{64,192},{128,0},{192,64},{1,129},{65,193},{129,1},{193,65... | collective-permute-start | bytes 786440 | tf_op jit(solution)/shard_map/ppermute | solution.py:381
  11.7 0.0 collective-permute-start.2
  11.7 0.5 collective-permute-start.3
  12.2 3.4 %collective-permute-start.4 = (bf16[16,128]{1,0:T(8,128)(2,1)S(1)}, bf16[16,128]{1,0:T(8,128)(2,1)S(1)}, u32[]{:S(2)}, u32[]{:S(2)}) collective-permute-start(bf16[16,128]{1,0:T(8,128)(2,1)S(1)} %get-tuple-element.29), channel_id=1, source_target_pairs={{0,128},{64,192},{128,0},{192,64},{1,129},{65,193},{129,1},{193,65... | collective-permute-start | bytes 12296 | tf_op jit(solution)/shard_map/ppermute | solution.py:381
  15.6 9.5 %collective-permute-done.3.q1 = bf16[16,128]{1,0:T(8,128)(2,1)S(1)} collective-permute-done((bf16[16,128]{1,0:T(8,128)(2,1)S(1)}, bf16[16,128]{1,0:T(8,128)(2,1)S(1)}, u32[]{:S(2)}, u32[]{:S(2)}) %collective-permute-start.3) | collective-permute-done | bytes 4128 | tf_op jit(solution)/shard_map/ppermute | solution.py:381
  25.0 0.0 collective-permute-start.5
  25.0 0.0 copy-done.1
  25.0 0.0 copy-done.7
  25.0 5.9 %local.1 = (bf16[1,16,1,512,256]{4,3,2,1,0:T(8,128)(2,1)}, bf16[16,512]{1,0:T(8,128)(2,1)S(1)}) custom-call(s32[48]{0:T(128)S(1)} %get-tuple-element.24.info, s32[16]{0:T(128)S(1)} %copy-done.7, f32[16,8,128]{2,1,0:T(8,128)S(1)} %get-tuple-element.34.q_slots, bf16[1,16,1,512,256]{4,3,2,1,0:T(8,128)(2,1)S(1)} %copy-done.1), custom_call_target="tpu_custom_call" | custom-call | tf_op jit(solution)/shard_map/local/pallas_call | solution.py:385
  30.9 0.0 collective-permute-done.4.q2
  30.9 0.0 collective-permute-done.5.q3
  30.9 0.0 copy-done.3
  30.9 0.0 copy-start.2
  30.9 3.4 %copy-done.2 = bf16[1,512,8192]{2,1,0:T(8,128)(2,1)S(1)} copy-done((bf16[1,512,8192]{2,1,0:T(8,128)(2,1)S(1)}, bf16[1,512,8192]{2,1,0:T(8,128)(2,1)}, u32[]{:S(2)}) %copy-start.2) | copy-done | bytes 8388632
  34.3 27.7 %chain.1 = (bf16[2,256,256]{2,1,0:T(8,128)(2,1)S(1)}, bf16[2,256,256]{2,1,0:T(8,128)(2,1)S(1)}, bf16[2,256,256]{2,1,0:T(8,128)(2,1)S(1)}, bf16[16,1024]{1,0:T(8,128)(2,1)S(1)}, s32[8,128]{1,0:T(8,128)S(1)}) custom-call(s32[48]{0:T(128)S(1)} %get-tuple-element.24.info, s32[16]{0:T(128)S(1)} %copy-done.7, bf16[16,128]{1,0:T(8,128)(2,1)S(1)} %collective-permute-done.3.q1, ...), custom_call_target="tpu_custom_call" | custom-call | tf_op jit(solution)/shard_map/chain/pallas_call | solution.py:396
  62.0 0.0 collective-permute-done.a1
  62.1 0.0 collective-permute-done.1.a2
  62.1 0.0 collective-permute-done.2.a3
  62.1 2.3 %place.1 = (bf16[1,16,1,512,256]{4,3,2,1,0:T(8,128)(2,1)}, bf16[1,16,1024]{2,1,0:T(8,128)(2,1)}, s32[16]{0:T(128)}) custom-call(s32[48]{0:T(128)S(1)} %get-tuple-element.24.info, bf16[2,256,256]{2,1,0:T(8,128)(2,1)S(1)} %collective-permute-done.a1, bf16[2,256,256]{2,1,0:T(8,128)(2,1)S(1)} %collective-permute-done.1.a2, ...), custom_call_target="tpu_custom_call", output_to_operand_aliasing={{0}: (9, {})} | custom-call | tf_op jit(solution)/shard_map/place/pallas_call | solution.py:419
Async XLA Ops:
  0.6 2.2 %copy-start = (bf16[1,16,1,512,256]{4,3,2,1,0:T(8,128)(2,1)S(1)}, bf16[1,16,1,512,256]{4,3,2,1,0:T(8,128)(2,1)}, u32[]{:S(2)}) copy-start(bf16[1,16,1,512,256]{4,3,2,1,0:T(8,128)(2,1)} %kv.3) | copy-start | bytes 12582916
  2.8 0.7 %copy-start.4 = (bf16[1,16,512]{2,1,0:T(8,128)(2,1)S(1)}, bf16[1,16,512]{2,1,0:T(8,128)(2,1)}, u32[]{:S(2)}) copy-start(bf16[1,16,512]{2,1,0:T(8,128)(2,1)} %q_ref.1) | copy-start | bytes 49156
  3.5 0.7 %copy-start.5 = (bf16[1,16,256]{2,1,0:T(8,128)(2,1)S(1)}, bf16[1,16,256]{2,1,0:T(8,128)(2,1)}, u32[]{:S(2)}) copy-start(bf16[1,16,256]{2,1,0:T(8,128)(2,1)} %new_ref.1) | copy-start | bytes 24580
  4.2 0.7 %copy-start.6 = (s32[16]{0:T(128)S(1)}, s32[16]{0:T(128)}, u32[]{:S(2)}) copy-start(s32[16]{0:T(128)} %lengths.5) | copy-start | bytes 196
  4.9 0.7 %copy-start.8 = (s32[64]{0:T(128)S(1)}, s32[64]{0:T(128)}, u32[]{:S(2)}) copy-start(s32[64]{0:T(128)} %anchor.1) | copy-start | bytes 772
  5.5 19.5 %copy-start.1 = (bf16[1,16,1,512,256]{4,3,2,1,0:T(8,128)(2,1)S(1)}, bf16[1,16,1,512,256]{4,3,2,1,0:T(8,128)(2,1)}, u32[]{:S(2)}) copy-start(bf16[1,16,1,512,256]{4,3,2,1,0:T(8,128)(2,1)} %kv.3) | copy-start | bytes 12582916
  5.5 19.5 %copy-start.7 = (s32[16]{0:T(128)S(1)}, s32[16]{0:T(128)}, u32[]{:S(2)}) copy-start(s32[16]{0:T(128)} %lengths.5) | copy-start | bytes 196
  5.6 25.4 %copy-start.3 = (bf16[16,1024]{1,0:T(8,128)(2,1)S(1)}, bf16[16,1024]{1,0:T(8,128)(2,1)}, u32[]{:S(2)}) copy-start(bf16[16,1024]{1,0:T(8,128)(2,1)} %hidden.1) | copy-start | bytes 98308
  9.3 52.8 %collective-permute-start = (bf16[2,256,256]{2,1,0:T(8,128)(2,1)S(1)}, bf16[2,256,256]{2,1,0:T(8,128)(2,1)S(1)}, u32[]{:S(2)}, u32[]{:S(2)}) collective-permute-start(bf16[2,256,256]{2,1,0:T(8,128)(2,1)S(1)} %get-tuple-element.25.a1), channel_id=1, source_target_pairs={{0,64},{64,128},{128,192},{192,0},{1,65},{65,129},{129,193},{193,1... | collective-permute-start | bytes 786440 | tf_op jit(solution)/shard_map/ppermute | solution.py:381
  9.5 52.5 %collective-permute-start.1 = (bf16[2,256,256]{2,1,0:T(8,128)(2,1)S(1)}, bf16[2,256,256]{2,1,0:T(8,128)(2,1)S(1)}, u32[]{:S(2)}, u32[]{:S(2)}) collective-permute-start(bf16[2,256,256]{2,1,0:T(8,128)(2,1)S(1)} %get-tuple-element.26.a2), channel_id=1, source_target_pairs={{0,128},{64,192},{128,0},{192,64},{1,129},{65,193},{129,1},{193,65... | collective-permute-start | bytes 786440 | tf_op jit(solution)/shard_map/ppermute | solution.py:381
  11.7 50.4 %collective-permute-start.2 = (bf16[2,256,256]{2,1,0:T(8,128)(2,1)S(1)}, bf16[2,256,256]{2,1,0:T(8,128)(2,1)S(1)}, u32[]{:S(2)}, u32[]{:S(2)}) collective-permute-start(bf16[2,256,256]{2,1,0:T(8,128)(2,1)S(1)} %get-tuple-element.27.a3), channel_id=1, source_target_pairs={{0,192},{64,0},{128,64},{192,128},{1,193},{65,1},{129,65},{193,129... | collective-permute-start | bytes 786440 | tf_op jit(solution)/shard_map/ppermute | solution.py:381
  11.7 13.3 %collective-permute-start.3 = (bf16[16,128]{1,0:T(8,128)(2,1)S(1)}, bf16[16,128]{1,0:T(8,128)(2,1)S(1)}, u32[]{:S(2)}, u32[]{:S(2)}) collective-permute-start(bf16[16,128]{1,0:T(8,128)(2,1)S(1)} %get-tuple-element.28), channel_id=1, source_target_pairs={{0,192},{64,0},{128,64},{192,128},{1,193},{65,1},{129,65},{193,129... | collective-permute-start | bytes 12296 | tf_op jit(solution)/shard_map/ppermute | solution.py:381
  12.2 18.7 %collective-permute-start.4 = (bf16[16,128]{1,0:T(8,128)(2,1)S(1)}, bf16[16,128]{1,0:T(8,128)(2,1)S(1)}, u32[]{:S(2)}, u32[]{:S(2)}) collective-permute-start(bf16[16,128]{1,0:T(8,128)(2,1)S(1)} %get-tuple-element.29), channel_id=1, source_target_pairs={{0,128},{64,192},{128,0},{192,64},{1,129},{65,193},{129,1},{193,65... | collective-permute-start | bytes 12296 | tf_op jit(solution)/shard_map/ppermute | solution.py:381
  25.0 5.9 %collective-permute-start.5 = (bf16[16,128]{1,0:T(8,128)(2,1)S(1)}, bf16[16,128]{1,0:T(8,128)(2,1)S(1)}, u32[]{:S(2)}, u32[]{:S(2)}) collective-permute-start(bf16[16,128]{1,0:T(8,128)(2,1)S(1)} %get-tuple-element.30), channel_id=1, source_target_pairs={{0,64},{64,128},{128,192},{192,0},{1,65},{65,129},{129,193},{193,1... | collective-permute-start | bytes 12296 | tf_op jit(solution)/shard_map/ppermute | solution.py:381
  30.9 3.4 %copy-start.2 = (bf16[1,512,8192]{2,1,0:T(8,128)(2,1)S(1)}, bf16[1,512,8192]{2,1,0:T(8,128)(2,1)}, u32[]{:S(2)}) copy-start(bf16[1,512,8192]{2,1,0:T(8,128)(2,1)} %weight.1) | copy-start | bytes 25165828

commit v2 on v1

v2 whole, which is shorter than its diff:
```python
import functools
import math

import jax
import jax.numpy as jnp
from jax import lax
from jax.experimental import pallas as pl
from jax.experimental.pallas import tpu as pltpu
from jax.sharding import PartitionSpec as P

MESH = pl.DeviceIdType.MESH
BF = jnp.bfloat16
F32 = jnp.float32
I32 = jnp.int32

INST = 4
TP = 8
SECTIONS = 8
SLOTS = 16
MIG = 2
GROUP = 4
HD = 128
CTX = 512
MODEL = 8192
COLS = MODEL // TP
CUT = 128
EARLY = 96
LATE = CTX - EARLY
SHIFTS = (1, 2, 3)
MOVES = len(SHIFTS) * MIG
STAY = SLOTS - MOVES
ORDER = (3, 5, 1, 7, 4, 2, 6)
INV_ROOT = 1.0 / math.sqrt(HD)

def wrap(value, count):
    return lax.rem(value + count, count)


def attend(queries, keys, values, lengths):
    scores = []
    for query, blocks in zip(queries, keys):
        rows = query.astype(BF)
        parts = [
            lax.dot_general(rows, block, (((1,), (1,)), ((), ())), preferred_element_type=F32) for block in blocks
        ]
        scores.append(jnp.concatenate(parts, axis=1))
    place = lax.broadcasted_iota(I32, (8, CTX), 1)
    probs = []
    for query, score, length in zip(queries, scores, lengths):
        score = jnp.where(place < length, score * INV_ROOT, -jnp.inf)
        new_score = jnp.sum(query * query[4:5, :], axis=1, keepdims=True) * INV_ROOT
        top = jnp.maximum(jnp.max(score, axis=1, keepdims=True), new_score)
        expo = jnp.exp(score - top)
        new_expo = jnp.exp(new_score - top)
        scale = 1.0 / (jnp.sum(expo, axis=1, keepdims=True) + new_expo)
        probs.append(((expo * scale).astype(BF), (new_expo * scale).astype(BF).astype(F32)))
    results = []
    for query, (prob, new_prob), blocks in zip(queries, probs, values):
        result = new_prob * query[5:6, :]
        start = 0
        for block in blocks:
            stop = start + block.shape[0]
            result = result + jnp.dot(prob[:, start:stop], block, preferred_element_type=F32)
            start = stop
        results.append(result)
    return results


def scan_leaving(anchor, me, shift):
    dest = wrap(me + shift, INST)
    count = jnp.int32(0)
    picked = [jnp.int32(0)] * MIG
    for slot in range(SLOTS):
        source = anchor[dest * SLOTS + slot]
        hit = lax.shift_right_logical(source, 4) == me
        for rank in range(MIG):
            picked[rank] = jnp.where(hit & (count == rank), source & (SLOTS - 1), picked[rank])
        count = count + hit.astype(I32)
    return picked


def scan_arriving(anchor, me):
    counts = [jnp.int32(0)] * len(SHIFTS)
    found = [jnp.int32(0)] * MOVES
    positions = []
    for slot in range(SLOTS):
        owner = lax.shift_right_logical(anchor[me * SLOTS + slot], 4)
        position = jnp.int32(-1)
        for at, shift in enumerate(SHIFTS):
            hit = owner == wrap(me - shift, INST)
            position = jnp.where(hit, at * MIG + jnp.minimum(counts[at], MIG - 1), position)
            for rank in range(MIG):
                one = at * MIG + rank
                found[one] = jnp.where(hit & (counts[at] == rank), slot, found[one])
            counts[at] = counts[at] + hit.astype(I32)
        positions.append(position)
    return positions, found


def scan_staying(anchor, me):
    rank = jnp.int32(0)
    slots = [jnp.int32(0)] * STAY
    for slot in range(SLOTS):
        hit = lax.shift_right_logical(anchor[me * SLOTS + slot], 4) == me
        for one in range(max(0, slot - MOVES), min(slot + 1, STAY)):
            slots[one] = jnp.where(hit & (rank == one), slot, slots[one])
        rank = rank + hit.astype(I32)
    return slots


def chain_kernel(
    anchor_in, lengths_in, q_in, new_in, hidden_in, kv, weight,
    kv_a, kv_b, early_in, late_in, out, moved_len,
    anchor, lengths, q_rows, new_rows, hidden, q_slots, table, w_blocks,
    asks, asks_in, early, late, back, back_in, tile, tile_in, rows_m,
    send_l, recv_l, send_m, recv_m, delta_l, part_l, delta_m, part_m, rows, acc_m,
    load_sems, w_sems, ask_sems, early_sems, back_sems, tile_sems, late_sems,
    l_sems, m_sems, pl_sems, pm_sems, ready,
):
    inst, section, tp = (lax.axis_index(name) for name in ("inst", "section", "tp"))
    far_half = lax.rem(tp, 2)

    def on_inst(shift):
        return {"inst": wrap(inst + shift, INST)}

    def on_tp(distance):
        return {"tp": wrap(tp + distance, TP)}

    def remote(source, target, sems, at, device):
        return pltpu.make_async_remote_copy(
            src_ref=source, dst_ref=target, send_sem=sems.at[0, at], recv_sem=sems.at[1, at],
            device_id=device, device_id_type=MESH,
        )

    def signal(sem, device):
        pl.semaphore_signal(sem, inc=1, device_id=device, device_id_type=MESH)

    barrier = pltpu.get_barrier_semaphore()
    for shift in SHIFTS:
        signal(barrier, on_inst(shift))
    for distance in (2, 4, 6):
        signal(barrier, on_tp(distance))
    for distance in range(1, SECTIONS):
        pl.when(section + distance < SECTIONS)(
            lambda distance=distance: signal(barrier, {"section": section + distance})
        )

    @pl.when(far_half == 0)
    def _():
        for distance in (1, 3, 5, 7):
            signal(barrier, on_tp(distance))

    small = [
        pltpu.make_async_copy(source, target, load_sems.at[at])
        for at, (source, target) in enumerate(
            (
                (anchor_in, anchor),
                (q_in, q_rows),
                (new_in, new_rows),
                (lengths_in, lengths),
                (hidden_in, hidden),
                (kv.at[0, :, 0, pl.ds(0, CUT)], kv_a),
                (kv.at[0, :, 0, pl.ds(CUT, CTX - CUT)], kv_b),
            )
        )
    ]
    for copy in small:
        copy.start()
    loads = {}
    for distance in ORDER + (0,):
        columns = pl.ds(pl.multiple_of(wrap(tp + distance, TP) * COLS, COLS), COLS)
        loads[distance] = pltpu.make_async_copy(
            weight.at[0, :, columns], w_blocks.at[distance], w_sems.at[distance]
        )
        loads[distance].start()

    small[1].wait()
    small[2].wait()
    queries = q_rows[0].astype(F32)
    pairs = new_rows[0].astype(F32)
    for head in range(GROUP):
        q_slots[:, head, :] = queries[:, head * HD : (head + 1) * HD]
    q_slots[:, 4, :] = pairs[:, :HD]
    q_slots[:, 5, :] = pairs[:, HD:]
    q_slots[:, 6, :] = jnp.zeros((SLOTS, HD), F32)
    q_slots[:, 7, :] = jnp.zeros((SLOTS, HD), F32)
    small[0].wait()
    positions, found = scan_arriving(anchor, inst)
    for at in range(len(SHIFTS)):
        asks[at] = jnp.concatenate([q_slots[found[at * MIG + rank]] for rank in range(MIG)], axis=0).astype(BF)
    leaving = [scan_leaving(anchor, inst, shift) for shift in SHIFTS]
    pl.semaphore_wait(barrier, len(SHIFTS) + 3 + section + 4 * far_half)
    ask_copies = [
        remote(asks.at[at], asks_in.at[at], ask_sems, at, on_inst(-shift)) for at, shift in enumerate(SHIFTS)
    ]
    for copy in ask_copies:
        copy.start()

    @pl.when(far_half == 1)
    def _():
        for distance in (1, 3, 5, 7):
            signal(ready.at[0], on_tp(distance))

    for distance in range(1, SECTIONS):
        pl.when(section >= distance)(
            lambda distance=distance: signal(ready.at[1], {"section": section - distance})
        )

    small[5].wait()
    early_copies, late_copies, back_copies, tile_copies = [], [], [], []
    for at, shift in enumerate(SHIFTS):
        early_copies.append(remote(early.at[at], early_in.at[at], early_sems, at, on_inst(shift)))
        late_copies.append(remote(late.at[at], late_in.at[at], late_sems, at, on_inst(shift)))
        back_copies.append(remote(back.at[at], back_in.at[at], back_sems, at, on_inst(shift)))
        tile_copies.append(remote(tile.at[at], tile_in.at[at], tile_sems, at, on_inst(shift)))
    for at in (1, 0, 2):
        for rank in range(MIG):
            early[at, rank] = kv_a[leaving[at][rank], :EARLY, :]
        early_copies[at].start()
    small[3].wait()
    small[6].wait()
    for at in range(len(SHIFTS)):
        for rank in range(MIG):
            slot = leaving[at][rank]
            late[at, rank, : CUT - EARLY, :] = kv_a[slot, EARLY:, :]
            late[at, rank, CUT - EARLY :, :] = kv_b[slot]

    def attend_at(queries, slots):
        return attend(
            queries,
            [[kv_a[slot, :, :HD], kv_b[slot, :, :HD]] for slot in slots],
            [[kv_a[slot, :, HD:], kv_b[slot, :, HD:]] for slot in slots],
            [lengths[slot] for slot in slots],
        )

    staying = scan_staying(anchor, inst)
    sources = [anchor[inst * SLOTS + slot] & (SLOTS - 1) for slot in staying]
    for one, result in enumerate(attend_at([q_slots[slot] for slot in staying], sources)):
        table[one] = result
    lane = lax.broadcasted_iota(I32, (8, 128), 1)
    for at in range(len(SHIFTS)):
        filled = jnp.zeros((8, 128), I32)
        for rank in range(MIG):
            filled = jnp.where(lane == rank, lengths[leaving[at][rank]], filled)
        tile[at] = filled

    asked = []
    for at in range(len(SHIFTS)):
        ask_copies[at].wait_recv()
        both = asks_in[at].astype(F32)
        asked += [both[rank * 8 : rank * 8 + 8, :] for rank in range(MIG)]
    results = attend_at(asked, [slot for pair in leaving for slot in pair])
    for at in range(len(SHIFTS)):
        back[at] = jnp.concatenate(results[at * MIG : at * MIG + MIG], axis=0).astype(BF)
        back_copies[at].start()
    for copy in tile_copies:
        copy.start()
    for at in (1, 0, 2):
        late_copies[at].start()

    for one in range(STAY, SLOTS):
        table[one] = jnp.zeros((8, HD), F32)
    stay = jnp.concatenate([table[:, head, :] for head in range(GROUP)], axis=1).astype(BF)

    @pl.when(far_half == 0)
    def _():
        pl.semaphore_wait(ready.at[0], 4)

    stay_copies = {}
    own_l = None
    for distance in ORDER + (0,):
        loads[distance].wait()
        share = jnp.dot(stay, w_blocks[distance], preferred_element_type=F32)
        if distance == 0:
            own_l = share
        else:
            send_l[distance] = share.astype(BF)
            copy = remote(send_l.at[distance], recv_l.at[distance], l_sems, distance, on_tp(distance))
            copy.start()
            stay_copies[distance] = copy

    for copy in back_copies:
        copy.wait_recv()
    for at in range(len(SHIFTS)):
        both = back_in[at].astype(F32)
        for rank in range(MIG):
            rows_m[at * MIG + rank] = both[rank * 8 : rank * 8 + 8, :]
    rows_m[6] = jnp.zeros((8, HD), F32)
    rows_m[7] = jnp.zeros((8, HD), F32)
    come = jnp.concatenate([rows_m[:, head, :] for head in range(GROUP)], axis=1).astype(BF)
    half = COLS // 2
    come_copies = {}
    own_m = None
    for distance in ORDER + (0,):
        share = jnp.dot(come, w_blocks[distance], preferred_element_type=F32)
        share = jnp.concatenate([share[:, :half], share[:, half:]], axis=0)
        if distance == 0:
            own_m = share
        else:
            send_m[distance] = share.astype(BF)
            copy = remote(send_m.at[distance], recv_m.at[distance], m_sems, distance, on_tp(distance))
            copy.start()
            come_copies[distance] = copy

    def later(source, target, sems, do):
        for distance in range(1, SECTIONS):

            @pl.when(section + distance < SECTIONS)
            def _(distance=distance):
                do(remote(source, target.at[distance], sems, distance, {"section": section + distance}))

    def start(copy):
        copy.start()

    def sent(copy):
        copy.wait_send()

    pl.when(section < SECTIONS - 1)(lambda: pl.semaphore_wait(ready.at[1], SECTIONS - 1 - section))
    total = own_l
    for distance in ORDER:
        stay_copies[distance].wait_recv()
        total = total + recv_l[distance].astype(F32)
    delta_l[...] = total.astype(BF)
    later(delta_l, part_l, pl_sems, start)
    rows[...] = total
    total = own_m
    for distance in ORDER:
        come_copies[distance].wait_recv()
        total = total + recv_m[distance].astype(F32)
    delta_m[...] = total.astype(BF)
    later(delta_m, part_m, pm_sems, start)
    acc_m[...] = total

    for copy in tile_copies:
        copy.wait_recv()
    lens = jnp.zeros((8, 128), I32)
    for slot in range(SLOTS):
        lens = jnp.where(lane == slot, lengths[anchor[inst * SLOTS + slot] & (SLOTS - 1)], lens)
    for at in range(len(SHIFTS)):
        for rank in range(MIG):
            value = jnp.sum(jnp.where(lane == rank, tile_in[at], 0), axis=1, keepdims=True)
            lens = jnp.where(lane == found[at * MIG + rank], value, lens)
    moved_len[...] = lens

    for distance in range(1, SECTIONS):

        @pl.when(section >= distance)
        def _(distance=distance):
            remote(delta_l, part_l.at[distance], pl_sems, distance, {"section": section}).wait_recv()
            rows[...] += part_l[distance].astype(F32)

    small[4].wait()
    for distance in range(1, SECTIONS):

        @pl.when(section >= distance)
        def _(distance=distance):
            remote(delta_m, part_m.at[distance], pm_sems, distance, {"section": section}).wait_recv()
            acc_m[...] += part_m[distance].astype(F32)

    low, high = acc_m.at[pl.ds(0, 8)], acc_m.at[pl.ds(8, 8)]
    rank = jnp.int32(0)
    lines = []
    for slot in range(SLOTS):
        position = positions[slot]
        place = pl.ds(jnp.maximum(position, 0), 1)
        moved_row = jnp.concatenate([low[place, :], high[place, :]], axis=1)
        stay_row = rows[pl.ds(jnp.minimum(rank, STAY - 1), 1), :]
        lines.append(jnp.where(position >= 0, moved_row, stay_row))
        rank = rank + (position < 0).astype(I32)
    out[...] = (hidden[...].astype(F32) + jnp.concatenate(lines, axis=0)).astype(BF)

    later(delta_l, part_l, pl_sems, sent)
    later(delta_m, part_m, pm_sems, sent)
    for copy in list(stay_copies.values()) + list(come_copies.values()) + back_copies + tile_copies + ask_copies:
        copy.wait_send()
    for copy in early_copies + late_copies:
        copy.wait()


def place_kernel(
    anchor_in, kv_a, kv_b, early_in, late_in, out_rows, lens, out, moved, moved_len, anchor, scalars, sems, more
):
    me = lax.axis_index("inst")
    first = [
        pltpu.make_async_copy(anchor_in, anchor, more.at[0]),
        pltpu.make_async_copy(lens, scalars, more.at[1]),
        pltpu.make_async_copy(out_rows, out.at[0], more.at[2]),
    ]
    for copy in first:
        copy.start()
    first[0].wait()
    positions, _ = scan_arriving(anchor, me)

    def each(do):
        for slot in range(SLOTS):
            source = anchor[me * SLOTS + slot] & (SLOTS - 1)
            position = positions[slot]

            def move(low, high, cut, slot=slot):
                target = moved.at[0, slot, 0]
                do(pltpu.make_async_copy(low, target.at[pl.ds(0, cut)], sems.at[0, slot]))
                do(pltpu.make_async_copy(high, target.at[pl.ds(cut, CTX - cut)], sems.at[1, slot]))

            @pl.when(position < 0)
            def _(source=source, move=move):
                move(kv_a.at[source], kv_b.at[source], CUT)

            @pl.when(position >= 0)
            def _(position=position, move=move):
                at, rank = lax.shift_right_logical(position, 1), position & 1
                move(early_in.at[at, rank], late_in.at[at, rank], EARLY)

    each(lambda copy: copy.start())
    first[1].wait()
    for slot in range(SLOTS):
        moved_len[slot] = scalars[0, slot]
    first[2].wait()
    each(lambda copy: copy.wait())


def specs(*spaces):
    return [pl.BlockSpec(memory_space=space) for space in spaces]


def body(hidden, queries, new_kv, kv_cache, lengths, anchor, out_weight):
    vmem, smem, hbm = pltpu.VMEM, pltpu.SMEM, pltpu.HBM
    dma = pltpu.SemaphoreType.DMA
    hidden, queries, new_kv, kv_cache, lengths, anchor, out_weight = (
        pltpu.with_memory_space_constraint(value, hbm)
        for value in (hidden, queries, new_kv, kv_cache, lengths, anchor, out_weight)
    )
    shapes = [
        ((SLOTS, CUT, 2 * HD), BF), ((SLOTS, CTX - CUT, 2 * HD), BF),
        ((3, MIG, EARLY, 2 * HD), BF), ((3, MIG, LATE, 2 * HD), BF),
        ((SLOTS, COLS), BF), ((8, 128), I32),
    ]
    half = COLS // 2
    made = pl.pallas_call(
        chain_kernel,
        out_shape=[vmem(*shape) for shape in shapes],
        in_specs=specs(*[hbm] * 7),
        out_specs=specs(*[vmem] * 6),
        scratch_shapes=[
            smem((INST * SLOTS,), I32), smem((SLOTS,), I32),
            vmem(queries.shape, BF), vmem(new_kv.shape, BF), vmem((SLOTS, COLS), BF),
            vmem((SLOTS, 8, HD), F32), vmem((SLOTS, 8, HD), F32),
            vmem((TP, GROUP * HD, COLS), BF),
            vmem((3, 16, HD), BF), vmem((3, 16, HD), BF),
            vmem((3, MIG, EARLY, 2 * HD), BF), vmem((3, MIG, LATE, 2 * HD), BF),
            vmem((3, 16, HD), BF), vmem((3, 16, HD), BF),
            vmem((3, 8, 128), I32), vmem((3, 8, 128), I32),
            vmem((8, 8, HD), F32),
            vmem((TP, 16, COLS), BF), vmem((TP, 16, COLS), BF),
            vmem((TP, 16, half), BF), vmem((TP, 16, half), BF),
            vmem((16, COLS), BF), vmem((SECTIONS, 16, COLS), BF),
            vmem((16, half), BF), vmem((SECTIONS, 16, half), BF),
            vmem((SLOTS, COLS), F32), vmem((16, half), F32),
            dma((7,)), dma((TP,)), dma((2, 3)), dma((2, 3)), dma((2, 3)), dma((2, 3)), dma((2, 3)),
            dma((2, TP)), dma((2, TP)), dma((2, SECTIONS)), dma((2, SECTIONS)),
            pltpu.SemaphoreType.REGULAR((2,)),
        ],
        compiler_params=pltpu.CompilerParams(
            collective_id=0, has_side_effects=True, vmem_limit_bytes=32 << 20
        ),
        name="chain",
    )(anchor, lengths, queries, new_kv, hidden, kv_cache, out_weight)
    out, moved, moved_len = pl.pallas_call(
        place_kernel,
        out_shape=[
            jax.ShapeDtypeStruct((1, SLOTS, COLS), BF),
            jax.ShapeDtypeStruct(kv_cache.shape, BF),
            jax.ShapeDtypeStruct((SLOTS,), I32),
        ],
        in_specs=specs(hbm, *[vmem] * 6),
        out_specs=specs(hbm, hbm, smem),
        scratch_shapes=[smem((INST * SLOTS,), I32), smem((8, 128), I32), dma((2, SLOTS)), dma((3,))],
        compiler_params=pltpu.CompilerParams(vmem_limit_bytes=8 << 20),
        name="place",
    )(anchor, *made)
    return out, moved, moved_len


def solution(mesh):
    return jax.shard_map(
        body,
        mesh=mesh,
        in_specs=(
            P("inst", "tp"),
            P("section", "inst", "tp"),
            P("section", "inst", "tp"),
            P("section", "inst", "tp", None, None),
            P("inst"),
            P(),
            P("section", "tp", None),
        ),
        out_specs=(P("section", "inst", "tp"), P("section", "inst", "tp", None, None), P("inst")),
        check_vma=False,
    )
```

time: 65.7 us -> 37 us (0.56); the launches traced: 64.4 us -> 37 us
  waiting for transfers between devices: 9.48 us -> 0 us
  local copies, waits for them, and re-layouts: 8.29 us -> 0 us
  starting transfers between devices: 6.29 us -> 0 us
  Pallas kernels: 39.6 us -> 36.3 us
    ppermute x6 -> x0, waiting for transfers between devices: 9.48 us -> none  [permute(): lax.ppermute(value, 'inst', [(i, (i + shift) % INST) for i in range(INST)])]
    unnamed x18 -> x0, local copies, waits for them, and re-layouts: 8.29 us -> none
    ppermute x6 -> x0, starting transfers between devices: 6.29 us -> none  [permute(): lax.ppermute(value, 'inst', [(i, (i + shift) % INST) for i in range(INST)])]
    pallas_call x4 -> x2, Pallas kernels: 39.6 us -> 36.3 us  [the longest x1 32.8 us: body(): pl.pallas_call(chain_kernel, out_shape=[vmem(*shape) for shape in shapes]...]
  transfers between devices with their start and end apart: 6 -> 0, of which waited for: 1 -> 0; matrix products, arithmetic and copies ran while one was open for 0% -> 0% of each run, Pallas kernels for 52% -> 0%
where the time goes in v2:
time: 37 us
  Pallas kernels  36.3 us (98%)
  between operations  0.64 us (2%)
    pallas_call x1, Pallas kernels, body(): pl.pallas_call(chain_kernel, out_shape=[vmem(*shape) for shape in shapes]...  32.8 us
    pallas_call x1, Pallas kernels, body(): pl.pallas_call(place_kernel, out_shape=[jax.ShapeDtypeStruct((1, SLOTS, C...  3.49 us

profile of v2, /device:TPU:103, one launch (start us, length us, event | category | flops | bytes accessed | tf_op | source)
XLA Modules:
  0.0 37.0 jit_solution(1501693227347092280)
XLA Ops:
  0.6 32.8 %chain.1 = (bf16[16,128,256]{2,1,0:T(8,128)(2,1)S(1)}, bf16[16,384,256]{2,1,0:T(8,128)(2,1)S(1)}, bf16[3,2,96,256]{3,2,1,0:T(8,128)(2,1)S(1)}, bf16[3,2,416,256]...) custom-call(s32[64]{0:T(128)} %anchor_in.3, s32[16]{0:T(128)} %lengths_in.1, ...), custom_call_target="tpu_custom_call" | custom-call | tf_op jit(solution)/shard_map/chain/pallas_call | solution.py:438
  33.5 3.5 %place.1 = (bf16[1,16,1024]{2,1,0:T(8,128)(2,1)}, bf16[1,16,1,512,256]{4,3,2,1,0:T(8,128)(2,1)}, s32[16]{0:T(128)}) custom-call(s32[64]{0:T(128)} %anchor_in.3, bf16[16,128,256]{2,1,0:T(8,128)(2,1)S(1)} %get-tuple-element.9.kv_a, bf16[16,384,256]{2,1,0:T(8,128)(2,1)S(1)} %get-tuple-element.10.kv_b, bf16[3,2,96,256]{3,2,1,0:T(8,128)(2,1)S(1)} %get-tuple-element.11.early_in, ...), custom_call_target="tpu_custom_call" | custom-call | tf_op jit(solution)/shard_map/place/pallas_call | solution.py:467

commit v3 on v2

--- a/solution.py
+++ b/solution.py
@@ -23,6 +23,8 @@
 CTX = 512
 MODEL = 8192
 COLS = MODEL // TP
+FOLD_L = (SLOTS - 6) * COLS // 16
+FOLD_M = 6 * COLS // 16
 CUT = 128
 EARLY = 96
 LATE = CTX - EARLY
@@ -34,6 +36,35 @@
 
 def wrap(value, count):
     return lax.rem(value + count, count)
+
+
+def fold_stay(rows):
+    step = COLS // 4
+    tail = jnp.concatenate([rows[8:10, k * step : (k + 1) * step] for k in range(4)], axis=0)
+    wide = jnp.concatenate([rows[:8], tail], axis=1)
+    return jnp.concatenate([wide[:, :FOLD_L], wide[:, FOLD_L:]], axis=0)
+
+
+def unfold_stay(folded):
+    wide = jnp.concatenate([folded[:8], folded[8:]], axis=1)
+    tail = jnp.concatenate([wide[2 * k : 2 * k + 2, COLS:] for k in range(4)], axis=1)
+    return wide[:, :COLS], tail
+
+
+def fold_come(rows):
+    step = COLS // 4
+    rest = [rows[k : k + 1, 3 * step :] for k in range(6)]
+    wide = jnp.concatenate(
+        [rows[:6, : 3 * step], jnp.concatenate(rest[:3], axis=1), jnp.concatenate(rest[3:], axis=1)], axis=0
+    )
+    return jnp.concatenate([wide[:, :FOLD_M], wide[:, FOLD_M:]], axis=0)
+
+
+def unfold_come(folded):
+    step = COLS // 4
+    wide = jnp.concatenate([folded[:8], folded[8:]], axis=1)
+    rest = [wide[6 + k // 3 : 7 + k // 3, (k % 3) * step : (k % 3 + 1) * step] for k in range(6)]
+    return jnp.concatenate([wide[:6], jnp.concatenate(rest, axis=0)], axis=1)
 
 
 def attend(queries, keys, values, lengths):
@@ -110,10 +141,10 @@
 
 def chain_kernel(
     anchor_in, lengths_in, q_in, new_in, hidden_in, kv, weight,
-    kv_a, kv_b, early_in, late_in, out, moved_len,
+    kv_a, kv_b, early_in, late_in, out, notes,
     anchor, lengths, q_rows, new_rows, hidden, q_slots, table, w_blocks,
     asks, asks_in, early, late, back, back_in, tile, tile_in, rows_m,
-    send_l, recv_l, send_m, recv_m, delta_l, part_l, delta_m, part_m, rows, acc_m,
+    send_l, recv_l, send_m, recv_m, delta_l, part_l, delta_m, part_m, rows, acc_m, lines_l, lines_m,
     load_sems, w_sems, ask_sems, early_sems, back_sems, tile_sems, late_sems,
     l_sems, m_sems, pl_sems, pm_sems, ready,
 ):
@@ -166,14 +197,6 @@
     ]
     for copy in small:
         copy.start()
-    loads = {}
-    for distance in ORDER + (0,):
-        columns = pl.ds(pl.multiple_of(wrap(tp + distance, TP) * COLS, COLS), COLS)
-        loads[distance] = pltpu.make_async_copy(
-            weight.at[0, :, columns], w_blocks.at[distance], w_sems.at[distance]
-        )
-        loads[distance].start()
-
     small[1].wait()
     small[2].wait()
     queries = q_rows[0].astype(F32)
@@ -219,6 +242,13 @@
         early_copies[at].start()
     small[3].wait()
     small[6].wait()
+    loads = {}
+    for distance in ORDER + (0,):
+        columns = pl.ds(pl.multiple_of(wrap(tp + distance, TP) * COLS, COLS), COLS)
+        loads[distance] = pltpu.make_async_copy(
+            weight.at[0, :, columns], w_blocks.at[distance], w_sems.at[distance]
+        )
+        loads[distance].start()
     for at in range(len(SHIFTS)):
         for rank in range(MIG):
             slot = leaving[at][rank]
@@ -270,7 +300,7 @@
     own_l = None
     for distance in ORDER + (0,):
         loads[distance].wait()
-        share = jnp.dot(stay, w_blocks[distance], preferred_element_type=F32)
+        share = fold_stay(jnp.dot(stay, w_blocks[distance], preferred_element_type=F32))
         if distance == 0:
             own_l = share
         else:
@@ -288,12 +318,10 @@
     rows_m[6] = jnp.zeros((8, HD), F32)
     rows_m[7] = jnp.zeros((8, HD), F32)
     come = jnp.concatenate([rows_m[:, head, :] for head in range(GROUP)], axis=1).astype(BF)
-    half = COLS // 2
     come_copies = {}
     own_m = None
     for distance in ORDER + (0,):
-        share = jnp.dot(come, w_blocks[distance], preferred_element_type=F32)
-        share = jnp.concatenate([share[:, :half], share[:, half:]], axis=0)
+        share = fold_come(jnp.dot(come, w_blocks[distance], preferred_element_type=F32))
         if distance == 0:
             own_m = share
         else:
@@ -334,13 +362,17 @@
     for copy in tile_copies:
         copy.wait_recv()
     lens = jnp.zeros((8, 128), I32)
-    for slot in range(SLOTS):
-        lens = jnp.where(lane == slot, lengths[anchor[inst * SLOTS + slot] & (SLOTS - 1)], lens)
+    plan = jnp.zeros((8, 128), I32)
+    for slot in range(SLOTS):
+        source = anchor[inst * SLOTS + slot] & (SLOTS - 1)
+        lens = jnp.where(lane == slot, lengths[source], lens)
+        plan = jnp.where(lane == slot, jnp.where(positions[slot] < 0, source, SLOTS + positions[slot]), plan)
     for at in range(len(SHIFTS)):
         for rank in range(MIG):
             value = jnp.sum(jnp.where(lane == rank, tile_in[at], 0), axis=1, keepdims=True)
             lens = jnp.where(lane == found[at * MIG + rank], value, lens)
-    moved_len[...] = lens
+    row = lax.broadcasted_iota(I32, (8, 128), 0)
+    notes[...] = jnp.where(row == 0, lens, plan)
 
     for distance in range(1, SECTIONS):
 
@@ -357,14 +389,14 @@
             remote(delta_m, part_m.at[distance], pm_sems, distance, {"section": section}).wait_recv()
             acc_m[...] += part_m[distance].astype(F32)
 
-    low, high = acc_m.at[pl.ds(0, 8)], acc_m.at[pl.ds(8, 8)]
+    lines_l[0:8], lines_l[8:10] = unfold_stay(rows[...])
+    lines_m[0:6] = unfold_come(acc_m[...])
     rank = jnp.int32(0)
     lines = []
     for slot in range(SLOTS):
         position = positions[slot]
-        place = pl.ds(jnp.maximum(position, 0), 1)
-        moved_row = jnp.concatenate([low[place, :], high[place, :]], axis=1)
-        stay_row = rows[pl.ds(jnp.minimum(rank, STAY - 1), 1), :]
+        moved_row = lines_m[pl.ds(jnp.maximum(position, 0), 1), :]
+        stay_row = lines_l[pl.ds(jnp.minimum(rank, STAY - 1), 1), :]
         lines.append(jnp.where(position >= 0, moved_row, stay_row))
         rank = rank + (position < 0).astype(I32)
     out[...] = (hidden[...].astype(F32) + jnp.concatenate(lines, axis=0)).astype(BF)
@@ -377,45 +409,38 @@
         copy.wait()
 
 
-def place_kernel(
-    anchor_in, kv_a, kv_b, early_in, late_in, out_rows, lens, out, moved, moved_len, anchor, scalars, sems, more
-):
-    me = lax.axis_index("inst")
+def place_kernel(kv_a, kv_b, early_in, late_in, out_rows, notes, out, moved, moved_len, plan, lens, sems):
     first = [
-        pltpu.make_async_copy(anchor_in, anchor, more.at[0]),
-        pltpu.make_async_copy(lens, scalars, more.at[1]),
-        pltpu.make_async_copy(out_rows, out.at[0], more.at[2]),
+        pltpu.make_async_copy(notes, plan, sems.at[0]),
+        pltpu.make_async_copy(out_rows, out.at[0], sems.at[1]),
     ]
     for copy in first:
         copy.start()
     first[0].wait()
-    positions, _ = scan_arriving(anchor, me)
-
-    def each(do):
-        for slot in range(SLOTS):
-            source = anchor[me * SLOTS + slot] & (SLOTS - 1)
-            position = positions[slot]
-
-            def move(low, high, cut, slot=slot):
-                target = moved.at[0, slot, 0]
-                do(pltpu.make_async_copy(low, target.at[pl.ds(0, cut)], sems.at[0, slot]))
-                do(pltpu.make_async_copy(high, target.at[pl.ds(cut, CTX - cut)], sems.at[1, slot]))
-
-            @pl.when(position < 0)
-            def _(source=source, move=move):
-                move(kv_a.at[source], kv_b.at[source], CUT)
-
-            @pl.when(position >= 0)
-            def _(position=position, move=move):
-                at, rank = lax.shift_right_logical(position, 1), position & 1
-                move(early_in.at[at, rank], late_in.at[at, rank], EARLY)
-
-    each(lambda copy: copy.start())
+    for slot in range(SLOTS):
+        place = plan[1, slot]
+
+        def move(low, high, cut, slot=slot):
+            target = moved.at[0, slot, 0]
+            pltpu.make_async_copy(low, target.at[pl.ds(0, cut)], sems.at[2]).start()
+            pltpu.make_async_copy(high, target.at[pl.ds(cut, CTX - cut)], sems.at[2]).start()
+
+        @pl.when(place < SLOTS)
+        def _(place=place, move=move):
+            move(kv_a.at[place], kv_b.at[place], CUT)
+
+        @pl.when(place >= SLOTS)
+        def _(place=place, move=move):
+            at, rank = lax.shift_right_logical(place - SLOTS, 1), place & 1
+            move(early_in.at[at, rank], late_in.at[at, rank], EARLY)
+
+    for slot in range(SLOTS):
+        lens[slot] = plan[0, slot]
+    last = pltpu.make_async_copy(lens, moved_len, sems.at[3])
+    last.start()
     first[1].wait()
-    for slot in range(SLOTS):
-        moved_len[slot] = scalars[0, slot]
-    first[2].wait()
-    each(lambda copy: copy.wait())
+    pltpu.make_async_copy(moved, moved, sems.at[2]).wait()
+    last.wait()
 
 
 def specs(*spaces):
@@ -434,7 +459,6 @@
         ((3, MIG, EARLY, 2 * HD), BF), ((3, MIG, LATE, 2 * HD), BF),
         ((SLOTS, COLS), BF), ((8, 128), I32),
     ]
-    half = COLS // 2
     made = pl.pallas_call(
         chain_kernel,
         out_shape=[vmem(*shape) for shape in shapes],
@@ -450,11 +474,12 @@
             vmem((3, 16, HD), BF), vmem((3, 16, HD), BF),
             vmem((3, 8, 128), I32), vmem((3, 8, 128), I32),
             vmem((8, 8, HD), F32),
-            vmem((TP, 16, COLS), BF), vmem((TP, 16, COLS), BF),
-            vmem((TP, 16, half), BF), vmem((TP, 16, half), BF),
-            vmem((16, COLS), BF), vmem((SECTIONS, 16, COLS), BF),
-            vmem((16, half), BF), vmem((SECTIONS, 16, half), BF),
-            vmem((SLOTS, COLS), F32), vmem((16, half), F32),
+            vmem((TP, 16, FOLD_L), BF), vmem((TP, 16, FOLD_L), BF),
+            vmem((TP, 16, FOLD_M), BF), vmem((TP, 16, FOLD_M), BF),
+            vmem((16, FOLD_L), BF), vmem((SECTIONS, 16, FOLD_L), BF),
+            vmem((16, FOLD_M), BF), vmem((SECTIONS, 16, FOLD_M), BF),
+            vmem((16, FOLD_L), F32), vmem((16, FOLD_M), F32),
+            vmem((STAY, COLS), F32), vmem((MOVES, COLS), F32),
             dma((7,)), dma((TP,)), dma((2, 3)), dma((2, 3)), dma((2, 3)), dma((2, 3)), dma((2, 3)),
             dma((2, TP)), dma((2, TP)), dma((2, SECTIONS)), dma((2, SECTIONS)),
             pltpu.SemaphoreType.REGULAR((2,)),
@@ -471,12 +496,12 @@
             jax.ShapeDtypeStruct(kv_cache.shape, BF),
             jax.ShapeDtypeStruct((SLOTS,), I32),
         ],
-        in_specs=specs(hbm, *[vmem] * 6),
-        out_specs=specs(hbm, hbm, smem),
-        scratch_shapes=[smem((INST * SLOTS,), I32), smem((8, 128), I32), dma((2, SLOTS)), dma((3,))],
+        in_specs=specs(*[vmem] * 6),
+        out_specs=specs(hbm, hbm, hbm),
+        scratch_shapes=[smem((8, 128), I32), smem((SLOTS,), I32), dma((4,))],
         compiler_params=pltpu.CompilerParams(vmem_limit_bytes=8 << 20),
         name="place",
-    )(anchor, *made)
+    )(*made)
     return out, moved, moved_len
 
 

time: 37 us -> 34.9 us (0.943)
  Pallas kernels: 36.3 us -> 34 us
    pallas_call x1, Pallas kernels: 32.8 us -> 31.3 us  [body(): pl.pallas_call(chain_kernel, out_shape=[vmem(*shape) for shape in shapes]...]
    pallas_call x1, Pallas kernels: 3.49 us -> 2.63 us  [body(): pl.pallas_call(place_kernel, out_shape=[jax.ShapeDtypeStruct((1, SLOTS, C...]
where the time goes in v3:
time: 34.9 us; the launch traced here: 34.6 us
  Pallas kernels  34 us (97%)
  between operations  0.64 us (2%)
    pallas_call x1, Pallas kernels, body(): pl.pallas_call(chain_kernel, out_shape=[vmem(*shape) for shape in shapes]...  31.3 us
    pallas_call x1, Pallas kernels, body(): pl.pallas_call(place_kernel, out_shape=[jax.ShapeDtypeStruct((1, SLOTS, C...  2.63 us

profile of v3, /device:TPU:103, one launch (start us, length us, event | category | flops | bytes accessed | tf_op | source)
XLA Modules:
  0.0 34.6 jit_solution(2053597094596216500)
XLA Ops:
  0.6 31.3 %chain.1 = (bf16[16,128,256]{2,1,0:T(8,128)(2,1)S(1)}, bf16[16,384,256]{2,1,0:T(8,128)(2,1)S(1)}, bf16[3,2,96,256]{3,2,1,0:T(8,128)(2,1)S(1)}, bf16[3,2,416,256]...) custom-call(s32[64]{0:T(128)} %anchor_in.1, s32[16]{0:T(128)} %lengths_in.1, ...), custom_call_target="tpu_custom_call" | custom-call | tf_op jit(solution)/shard_map/chain/pallas_call | solution.py:462
  32.0 2.6 %place.1 = (bf16[1,16,1024]{2,1,0:T(8,128)(2,1)}, bf16[1,16,1,512,256]{4,3,2,1,0:T(8,128)(2,1)}, s32[16]{0:T(128)}) custom-call(bf16[16,128,256]{2,1,0:T(8,128)(2,1)S(1)} %get-tuple-element.9.kv_a, bf16[16,384,256]{2,1,0:T(8,128)(2,1)S(1)} %get-tuple-element.10.kv_b, bf16[3,2,96,256]{3,2,1,0:T(8,128)(2,1)S(1)} %get-tuple-element.11.early_in, ...), custom_call_target="tpu_custom_call" | custom-call | tf_op jit(solution)/shard_map/place/pallas_call | solution.py:492

commit v4 on v3

--- a/solution.py
+++ b/solution.py
@@ -25,8 +25,7 @@
 COLS = MODEL // TP
 FOLD_L = (SLOTS - 6) * COLS // 16
 FOLD_M = 6 * COLS // 16
-CUT = 128
-EARLY = 96
+EARLY = 128
 LATE = CTX - EARLY
 SHIFTS = (1, 2, 3)
 MOVES = len(SHIFTS) * MIG
@@ -149,7 +148,8 @@
     l_sems, m_sems, pl_sems, pm_sems, ready,
 ):
     inst, section, tp = (lax.axis_index(name) for name in ("inst", "section", "tp"))
-    far_half = lax.rem(tp, 2)
+    far_half, row = lax.rem(tp, 2), lax.div(tp, 2)
+    last = far_half * lax.div(row, TP // 2 - 1)
 
     def on_inst(shift):
         return {"inst": wrap(inst + shift, INST)}
@@ -169,18 +169,6 @@
     barrier = pltpu.get_barrier_semaphore()
     for shift in SHIFTS:
         signal(barrier, on_inst(shift))
-    for distance in (2, 4, 6):
-        signal(barrier, on_tp(distance))
-    for distance in range(1, SECTIONS):
-        pl.when(section + distance < SECTIONS)(
-            lambda distance=distance: signal(barrier, {"section": section + distance})
-        )
-
-    @pl.when(far_half == 0)
-    def _():
-        for distance in (1, 3, 5, 7):
-            signal(barrier, on_tp(distance))
-
     small = [
         pltpu.make_async_copy(source, target, load_sems.at[at])
         for at, (source, target) in enumerate(
@@ -190,13 +178,20 @@
                 (new_in, new_rows),
                 (lengths_in, lengths),
                 (hidden_in, hidden),
-                (kv.at[0, :, 0, pl.ds(0, CUT)], kv_a),
-                (kv.at[0, :, 0, pl.ds(CUT, CTX - CUT)], kv_b),
+                (kv.at[0, :, 0, pl.ds(0, EARLY)], kv_a),
+                (kv.at[0, :, 0, pl.ds(EARLY, CTX - EARLY)], kv_b),
             )
         )
     ]
     for copy in small:
         copy.start()
+    for step in (1, 2, 3):
+        pl.when(row + step < TP // 2)(lambda step=step: signal(barrier, {"tp": tp + 2 * step}))
+    for step in range(1, SECTIONS):
+        pl.when(section + step < SECTIONS)(lambda step=step: signal(barrier, {"section": section + step}))
+
+    pl.when(far_half == 0)(lambda: signal(barrier, {"tp": TP - 1}))
+
     small[1].wait()
     small[2].wait()
     queries = q_rows[0].astype(F32)
@@ -212,22 +207,6 @@
     for at in range(len(SHIFTS)):
         asks[at] = jnp.concatenate([q_slots[found[at * MIG + rank]] for rank in range(MIG)], axis=0).astype(BF)
     leaving = [scan_leaving(anchor, inst, shift) for shift in SHIFTS]
-    pl.semaphore_wait(barrier, len(SHIFTS) + 3 + section + 4 * far_half)
-    ask_copies = [
-        remote(asks.at[at], asks_in.at[at], ask_sems, at, on_inst(-shift)) for at, shift in enumerate(SHIFTS)
-    ]
-    for copy in ask_copies:
-        copy.start()
-
-    @pl.when(far_half == 1)
-    def _():
-        for distance in (1, 3, 5, 7):
-            signal(ready.at[0], on_tp(distance))
-
-    for distance in range(1, SECTIONS):
-        pl.when(section >= distance)(
-            lambda distance=distance: signal(ready.at[1], {"section": section - distance})
-        )
 
     small[5].wait()
     early_copies, late_copies, back_copies, tile_copies = [], [], [], []
@@ -236,10 +215,29 @@
         late_copies.append(remote(late.at[at], late_in.at[at], late_sems, at, on_inst(shift)))
         back_copies.append(remote(back.at[at], back_in.at[at], back_sems, at, on_inst(shift)))
         tile_copies.append(remote(tile.at[at], tile_in.at[at], tile_sems, at, on_inst(shift)))
+    for at in range(len(SHIFTS)):
+        for rank in range(MIG):
+            early[at, rank] = kv_a[leaving[at][rank]]
+    pl.semaphore_wait(barrier, len(SHIFTS) + row + section + last * (TP // 2))
+    ask_copies = [
+        remote(asks.at[at], asks_in.at[at], ask_sems, at, on_inst(-shift)) for at, shift in enumerate(SHIFTS)
+    ]
+    for copy in ask_copies:
+        copy.start()
+
     for at in (1, 0, 2):
-        for rank in range(MIG):
-            early[at, rank] = kv_a[leaving[at][rank], :EARLY, :]
         early_copies[at].start()
+
+    @pl.when(last == 1)
+    def _():
+        for step in range(TP // 2):
+            signal(ready.at[0], {"tp": 2 * step})
+
+    for step in (1, 2, 3):
+        pl.when(row >= step)(lambda step=step: signal(ready.at[0], {"tp": tp - 2 * step}))
+    for step in range(1, SECTIONS):
+        pl.when(section >= step)(lambda step=step: signal(ready.at[1], {"section": section - step}))
+
     small[3].wait()
     small[6].wait()
     loads = {}
@@ -252,8 +250,7 @@
     for at in range(len(SHIFTS)):
         for rank in range(MIG):
             slot = leaving[at][rank]
-            late[at, rank, : CUT - EARLY, :] = kv_a[slot, EARLY:, :]
-            late[at, rank, CUT - EARLY :, :] = kv_b[slot]
+            late[at, rank] = kv_b[slot]
 
     def attend_at(queries, slots):
         return attend(
@@ -292,9 +289,8 @@
         table[one] = jnp.zeros((8, HD), F32)
     stay = jnp.concatenate([table[:, head, :] for head in range(GROUP)], axis=1).astype(BF)
 
-    @pl.when(far_half == 0)
-    def _():
-        pl.semaphore_wait(ready.at[0], 4)
+    unheard = TP // 2 - 1 - row + 1 - far_half
+    pl.when(unheard > 0)(lambda: pl.semaphore_wait(ready.at[0], unheard))
 
     stay_copies = {}
     own_l = None
@@ -427,7 +423,7 @@
 
         @pl.when(place < SLOTS)
         def _(place=place, move=move):
-            move(kv_a.at[place], kv_b.at[place], CUT)
+            move(kv_a.at[place], kv_b.at[place], EARLY)
 
         @pl.when(place >= SLOTS)
         def _(place=place, move=move):
@@ -455,7 +451,7 @@
         for value in (hidden, queries, new_kv, kv_cache, lengths, anchor, out_weight)
     )
     shapes = [
-        ((SLOTS, CUT, 2 * HD), BF), ((SLOTS, CTX - CUT, 2 * HD), BF),
+        ((SLOTS, EARLY, 2 * HD), BF), ((SLOTS, CTX - EARLY, 2 * HD), BF),
         ((3, MIG, EARLY, 2 * HD), BF), ((3, MIG, LATE, 2 * HD), BF),
         ((SLOTS, COLS), BF), ((8, 128), I32),
     ]

time: 34.9 us -> 34 us (0.974)
  Pallas kernels: 34 us -> 33.2 us
    pallas_call x1, Pallas kernels: 31.3 us -> 30.6 us  [body(): pl.pallas_call(chain_kernel, out_shape=[vmem(*shape) for shape in shapes]...]
where the time goes in v4:
time: 34 us; the launch traced here: 33.9 us
  Pallas kernels  33.2 us (98%)
  between operations  0.64 us (2%)
    pallas_call x1, Pallas kernels, body(): pl.pallas_call(chain_kernel, out_shape=[vmem(*shape) for shape in shapes]...  30.6 us
    pallas_call x1, Pallas kernels, body(): pl.pallas_call(place_kernel, out_shape=[jax.ShapeDtypeStruct((1, SLOTS, C...  2.63 us

profile of v4, /device:TPU:103, one launch (start us, length us, event | category | flops | bytes accessed | tf_op | source)
XLA Modules:
  0.0 33.9 jit_solution(8511046889231968598)
XLA Ops:
  0.6 30.6 %chain.1 = (bf16[16,128,256]{2,1,0:T(8,128)(2,1)S(1)}, bf16[16,384,256]{2,1,0:T(8,128)(2,1)S(1)}, bf16[3,2,128,256]{3,2,1,0:T(8,128)(2,1)S(1)}, bf16[3,2,384,256...) custom-call(s32[64]{0:T(128)} %anchor_in.1, s32[16]{0:T(128)} %lengths_in.1, ...), custom_call_target="tpu_custom_call" | custom-call | tf_op jit(solution)/shard_map/chain/pallas_call | solution.py:458
  31.2 2.6 %place.1 = (bf16[1,16,1024]{2,1,0:T(8,128)(2,1)}, bf16[1,16,1,512,256]{4,3,2,1,0:T(8,128)(2,1)}, s32[16]{0:T(128)}) custom-call(bf16[16,128,256]{2,1,0:T(8,128)(2,1)S(1)} %get-tuple-element.9.kv_a, bf16[16,384,256]{2,1,0:T(8,128)(2,1)S(1)} %get-tuple-element.10.kv_b, bf16[3,2,128,256]{3,2,1,0:T(8,128)(2,1)S(1)} %get-tuple-element.11.early_in, ...), custom_call_target="tpu_custom_call" | custom-call | tf_op jit(solution)/shard_map/place/pallas_call | solution.py:488

commit v5 on v4

--- a/solution.py
+++ b/solution.py
@@ -218,6 +218,13 @@
     for at in range(len(SHIFTS)):
         for rank in range(MIG):
             early[at, rank] = kv_a[leaving[at][rank]]
+    small[3].wait()
+    lane = lax.broadcasted_iota(I32, (8, 128), 1)
+    for at in range(len(SHIFTS)):
+        filled = jnp.zeros((8, 128), I32)
+        for rank in range(MIG):
+            filled = jnp.where(lane == rank, lengths[leaving[at][rank]], filled)
+        tile[at] = filled
     pl.semaphore_wait(barrier, len(SHIFTS) + row + section + last * (TP // 2))
     ask_copies = [
         remote(asks.at[at], asks_in.at[at], ask_sems, at, on_inst(-shift)) for at, shift in enumerate(SHIFTS)
@@ -227,6 +234,8 @@
 
     for at in (1, 0, 2):
         early_copies[at].start()
+    for copy in tile_copies:
+        copy.start()
 
     @pl.when(last == 1)
     def _():
@@ -238,7 +247,6 @@
     for step in range(1, SECTIONS):
         pl.when(section >= step)(lambda step=step: signal(ready.at[1], {"section": section - step}))
 
-    small[3].wait()
     small[6].wait()
     loads = {}
     for distance in ORDER + (0,):
@@ -264,12 +272,6 @@
     sources = [anchor[inst * SLOTS + slot] & (SLOTS - 1) for slot in staying]
     for one, result in enumerate(attend_at([q_slots[slot] for slot in staying], sources)):
         table[one] = result
-    lane = lax.broadcasted_iota(I32, (8, 128), 1)
-    for at in range(len(SHIFTS)):
-        filled = jnp.zeros((8, 128), I32)
-        for rank in range(MIG):
-            filled = jnp.where(lane == rank, lengths[leaving[at][rank]], filled)
-        tile[at] = filled
 
     asked = []
     for at in range(len(SHIFTS)):
@@ -280,8 +282,6 @@
     for at in range(len(SHIFTS)):
         back[at] = jnp.concatenate(results[at * MIG : at * MIG + MIG], axis=0).astype(BF)
         back_copies[at].start()
-    for copy in tile_copies:
-        copy.start()
     for at in (1, 0, 2):
         late_copies[at].start()
 

time: 34 us -> 37.9 us (1.11)
  the two profiles are of different devices: /device:TPU:103 before, /device:TPU:1 now
where the time goes in v5:
time: 37.9 us
  Pallas kernels  37.2 us (98%)
  between operations  0.64 us (2%)
    pallas_call x1, Pallas kernels, body(): pl.pallas_call(chain_kernel, out_shape=[vmem(*shape) for shape in shapes]...  34.6 us
    pallas_call x1, Pallas kernels, body(): pl.pallas_call(place_kernel, out_shape=[jax.ShapeDtypeStruct((1, SLOTS, C...  2.63 us

profile of v5, /device:TPU:1, one launch (start us, length us, event | category | flops | bytes accessed | tf_op | source)
XLA Modules:
  0.0 37.9 jit_solution(7630835266186361004)
XLA Ops:
  0.6 34.6 %chain.1 = (bf16[16,128,256]{2,1,0:T(8,128)(2,1)S(1)}, bf16[16,384,256]{2,1,0:T(8,128)(2,1)S(1)}, bf16[3,2,128,256]{3,2,1,0:T(8,128)(2,1)S(1)}, bf16[3,2,384,256...) custom-call(s32[64]{0:T(128)} %anchor_in.1, s32[16]{0:T(128)} %lengths_in.1, ...), custom_call_target="tpu_custom_call" | custom-call | tf_op jit(solution)/shard_map/chain/pallas_call | solution.py:458
  35.2 2.6 %place.1 = (bf16[1,16,1024]{2,1,0:T(8,128)(2,1)}, bf16[1,16,1,512,256]{4,3,2,1,0:T(8,128)(2,1)}, s32[16]{0:T(128)}) custom-call(bf16[16,128,256]{2,1,0:T(8,128)(2,1)S(1)} %get-tuple-element.9.kv_a, bf16[16,384,256]{2,1,0:T(8,128)(2,1)S(1)} %get-tuple-element.10.kv_b, bf16[3,2,128,256]{3,2,1,0:T(8,128)(2,1)S(1)} %get-tuple-element.11.early_in, ...), custom_call_target="tpu_custom_call" | custom-call | tf_op jit(solution)/shard_map/place/pallas_call | solution.py:488
